TPU v7x, 256 devices: a whole 4x4x8 slice. The times are simulated.
256 devices in a mesh: blk: 64 (over x, z, core), rep: 4 (over y).
Axes of the slice: x: 4, y: 4, z: 8, core: 2. Of those that a mesh axis runs over, the one named last changes fastest.
Arguments:
- amplitudes: bfloat16 [256, 196608], P(None, ('blk', 'rep')), may hold values from -6 to 6
- panels: bfloat16 [11008, 192, 768], P(('blk', 'rep')), may hold values from -0.21875 to 0.21875
- panel_owner_index: int32 [11008, 1], P(('blk', 'rep')), may hold values from 0 to 63; in each aligned block of 43 rows (0 to 42, 43 to 85, ...) at most 2 rows name the same one
- panel_target_tile: int32 [11008], P(('blk', 'rep')), may hold values from 0 to 15
- panel_tile_mask: int32 [11008, 4], P(('blk', 'rep')), may hold values 0 or 1
- tile_sizes: int32 [1024], replicated, may hold values from 64 to 192
- tile_irreps: int32 [1024], replicated, may hold values from 0 to 1
- occ_energy: float32 [256], P('rep'), may hold values from -3 to -0.5
- vir_energy: float32 [196608], P('blk'), may hold values from 0.5 to 6
Outputs:
- doubles_update: bfloat16 [256, 196608], P('rep', 'blk')
Inputs may be any that keep to these rules, and one draw needn't show every extreme that they name: `panel_owner_index`: within the 43 rows of one device no index of blk is named more than 2 times, a bound that some block reaches.
All inputs are finite; a program needn't handle non-finite values. No bound on the sum of `panel_tile_mask` on one device may be relied on, other than what follows from the above.
Results may differ from a plain program's by a relative error of at most 0.0049.
Values may be sent and summed in bfloat16 or wider, within the bound.
A program may use at most 128 MiB of HBM per device.

v0:
```python
import jax
import jax.numpy as jnp
from jax import lax
from jax.sharding import PartitionSpec as P


def shards(
    amplitudes,
    panels,
    panel_owner_index,
    panel_target_tile,
    panel_tile_mask,
    tile_sizes,
    tile_irreps,
    occ_energy,
    vir_energy,
):
    blk_count = lax.axis_size("blk")
    rep_count = lax.axis_size("rep")
    device = lax.axis_index("blk") * rep_count + lax.axis_index("rep")
    blk_index = lax.axis_index("blk")
    slot_count, tile_width, k_columns = panels.shape
    tiles_here = k_columns // tile_width
    row_count = amplitudes.shape[0]
    owned_tiles = tiles_here * rep_count
    capacity = max(2, (2 * slot_count + blk_count - 1) // blk_count)
    in_tile = jnp.arange(tile_width, dtype=jnp.int32)
    sizes_here = lax.dynamic_slice_in_dim(tile_sizes, device * tiles_here, tiles_here, 0)
    keep_cols = (in_tile[None, :] < sizes_here[:, None]).reshape(k_columns).astype(jnp.bfloat16)
    amp_live = amplitudes * keep_cols[None, :]
    owners = panel_owner_index[:, 0]
    tile_target = owners * owned_tiles + panel_target_tile
    irrep_source = lax.dynamic_slice_in_dim(tile_irreps, device * tiles_here, tiles_here, 0)
    irrep_target = tile_irreps[tile_target]
    live_blocks = (
        panel_tile_mask * (irrep_source[None, :] == irrep_target[:, None]).astype(jnp.int32)
    ).astype(jnp.bfloat16)
    panel_live = (
        panels.reshape(slot_count, tile_width, tiles_here, tile_width)
        * live_blocks[:, None, :, None]
    ).reshape(slot_count, tile_width, k_columns)
    partial_value = jnp.einsum(
        "slk,rk->slr", panel_live, amp_live, preferred_element_type=jnp.float32
    ).astype(jnp.bfloat16)
    order = jnp.arange(slot_count, dtype=jnp.int32)
    same_owner = (owners[:, None] == owners[None, :]) & (order[:, None] > order[None, :])
    slot_rank = jnp.sum(same_owner.astype(jnp.int32), axis=1)
    position = owners * capacity + slot_rank
    outbox = (
        jnp.zeros((blk_count * capacity, tile_width, row_count), jnp.bfloat16)
        .at[position]
        .set(partial_value)
    )
    outbox_ids = (
        jnp.full((blk_count * capacity,), owned_tiles, jnp.int32)
        .at[position]
        .set(panel_target_tile)
    )
    tile_ids = lax.all_to_all(outbox_ids, "blk", split_axis=0, concat_axis=0, tiled=True)
    tile_range = jnp.arange(owned_tiles, dtype=jnp.int32)
    received = lax.all_to_all(
        lax.all_to_all(outbox, "blk", split_axis=0, concat_axis=0, tiled=True),
        "rep",
        split_axis=2,
        concat_axis=0,
        tiled=True,
    )
    all_ids = lax.all_gather(tile_ids, "rep", axis=0, tiled=True)
    onehot = (all_ids[:, None] == tile_range[None, :]).astype(jnp.bfloat16)
    summed = jnp.einsum("mt,mcr->tcr", onehot, received, preferred_element_type=jnp.float32)
    shares = summed.reshape(owned_tiles * tile_width, row_count // rep_count)
    sizes_owned = lax.dynamic_slice_in_dim(tile_sizes, blk_index * owned_tiles, owned_tiles, 0)
    keep_out = (in_tile[None, :] < sizes_owned[:, None]).reshape(owned_tiles * tile_width)
    ladder_rows = shares.T
    denominator = occ_energy[:, None] - vir_energy[None, :]
    result = jnp.where(keep_out[None, :], ladder_rows / denominator, jnp.zeros_like(ladder_rows))
    return result.astype(jnp.bfloat16)


def solution(mesh):
    return jax.shard_map(
        shards,
        mesh=mesh,
        in_specs=(
            P(None, ("blk", "rep")),
            P(("blk", "rep"), None, None),
            P(("blk", "rep"), None),
            P(("blk", "rep")),
            P(("blk", "rep"), None),
            P(),
            P(),
            P("rep"),
            P("blk"),
        ),
        out_specs=P("rep", "blk"),
        check_vma=False,
    )
```

profile of v0, /device:TPU:1, one launch (start us, length us, event | category | flops | bytes accessed | tf_op | source)
XLA Modules:
  0.0 504.2 jit_solution(4351953480227384322)
XLA Ops:
  0.0 0.7 compare_select_fusion
  0.7 0.8 dynamic_slice.10
  1.5 1.5 gather_fusion
  2.9 0.8 select_convert_fusion
  3.7 0.1 copy.27
  3.8 0.1 mul.55
  3.9 0.1 mul.56
  4.0 0.8 dynamic_slice.11
  4.8 0.1 fusion.18
  4.9 0.1 reshape.49
  5.0 0.9 convert_reduce_fusion
  5.9 0.7 fusion.19
  6.5 10.1 %fusion.6 = bf16[43,192,256]{2,1,0:T(8,128)(2,1)} fusion(bf16[43,192,768]{2,1,0:T(8,128)(2,1)} %param.10, bf16[43,768]{1,0:T(8,128)(2,1)S(1)} %mul.56, bf16[256,768]{1,0:T(8,128)(2,1)} %param.9, bf16[768]{0:T(1024)(128)(2,1)S(1)} %reshape.49), kind=kOutput, calls=%fused_computation.9 | convolution fusion | flops 3255042048 | bytes 17369088 | tf_op jit(solution)/shard_map/slk,rk->slr/dot_general | solution.py:42
  16.6 6.0 %broadcast_in_dim.15 = bf16[128,192,256]{2,1,0:T(8,128)(2,1)} broadcast(bf16[]{:T(256)} %constant.7.clone.1), dimensions={} | broadcast | bytes 12582914 | tf_op jit(solution)/shard_map/broadcast_in_dim | solution.py:50
  22.6 14.9 %scatter_fusion = bf16[128,192,256]{2,1,0:T(8,128)(2,1)} fusion(bf16[128,192,256]{2,1,0:T(8,128)(2,1)} %broadcast_in_dim.15, s32[43]{0:T(128)S(1)} %fusion.19, bf16[43,192,256]{2,1,0:T(8,128)(2,1)} %fusion.6), kind=kCustom, calls=%fused_computation.2 | custom fusion | bytes 12681388 | tf_op jit(solution)/shard_map/scatter | solution.py:52
  37.6 13.1 %all-to-all-start.1 = ((bf16[128,192,256]{2,1,0:T(8,128)(2,1)}), bf16[128,192,256]{2,1,0:T(8,128)(2,1)}, u32[]{:S(2)}, u32[]{:S(2)}) async-start(bf16[128,192,256]{2,1,0:T(8,128)(2,1)} %scatter_fusion), calls=%async_computation.1 | async-start | bytes 25165824 | tf_op jit(solution)/shard_map/all_to_all | solution.py:62
  50.6 0.8 scatter_custom_fusion
  51.5 0.8 all_to_all.24
  52.2 274.1 %all-to-all-done.1 = bf16[128,192,256]{2,1,0:T(8,128)(2,1)} async-done(((bf16[128,192,256]{2,1,0:T(8,128)(2,1)}), bf16[128,192,256]{2,1,0:T(8,128)(2,1)}, u32[]{:S(2)}, u32[]{:S(2)}) %all-to-all-start.1) | async-done | bytes 12582944 | tf_op jit(solution)/shard_map/all_to_all | solution.py:62
  326.3 5.9 %all-to-all-start = ((s32[64,2,1]{1,2,0:T(1,128)}), s32[64,2,1]{1,2,0:T(1,128)S(1)}, u32[]{:S(2)}, u32[]{:S(2)}) async-start(s32[64,2,1]{1,2,0:T(1,128)} %bitcast.3), calls=%async_computation | async-start | bytes 65536 | tf_op jit(solution)/shard_map/all_to_all | solution.py:59
  332.3 18.1 %copy.28 = bf16[128,192,256]{0,1,2:T(8,128)(2,1)} copy(bf16[128,192,256]{2,1,0:T(8,128)(2,1)} %all-to-all-done.1) | data formatting | bytes 25165824 | tf_op jit(solution)/shard_map/all_to_all | solution.py:62
  350.4 6.3 %all-to-all-start.2 = ((bf16[128,192,256]{0,1,2:T(8,128)(2,1)}), bf16[128,192,256]{0,1,2:T(8,128)(2,1)}, u32[]{:S(2)}, u32[]{:S(2)}) async-start(bf16[128,192,256]{0,1,2:T(8,128)(2,1)} %copy.28), calls=%async_computation.2 | async-start | bytes 25165824 | tf_op jit(solution)/shard_map/all_to_all | solution.py:61
  356.8 0.8 dynamic_slice.9
  357.5 0.1 iota_compare_fusion.2
  357.6 0.1 lt.58
  357.7 0.5 broadcast.45
  358.2 0.7 reduce.3
  358.9 0.1 reshape.75
  359.1 137.5 %all-gather = s32[4,1,128]{2,1,0:T(1,128)S(1)} all-gather(s32[1,1,128]{2,1,0:T(1,128)S(1)} %reshape.75), channel_id=1, replica_groups=mesh['blk'=64,'rep'=4] {'rep'}, dimensions={0}, use_global_device_ids=true | all-gather | bytes 2560 | tf_op jit(solution)/shard_map/all_gather | solution.py:68
  496.5 6.3 %fusion.2 = f32[16,192,64]{1,0,2:T(8,128)S(1)} fusion(bf16[4,64,24,8,128]{4,3,2,1,0:T(8,128)(2,1)} %bitcast.11, s32[512]{0:T(512)S(1)} %bitcast.32), kind=kOutput, calls=%fused_computation.5 | convolution fusion | flops 201334784 | bytes 13371392 | tf_op jit(solution)/shard_map/mt,mcr->tcr/dot_general | solution.py:70
  502.9 0.4 reshape.48
  503.3 0.9 fusion.10
  (7 shorter events, 0.0 us)
Async XLA Ops:
  37.6 288.8 %all-to-all-start.1 = ((bf16[128,192,256]{2,1,0:T(8,128)(2,1)}), bf16[128,192,256]{2,1,0:T(8,128)(2,1)}, u32[]{:S(2)}, u32[]{:S(2)}) async-start(bf16[128,192,256]{2,1,0:T(8,128)(2,1)} %scatter_fusion), calls=%async_computation.1 | async-start | bytes 25165824 | tf_op jit(solution)/shard_map/all_to_all | solution.py:62
  326.3 24.1 %all-to-all-start = ((s32[64,2,1]{1,2,0:T(1,128)}), s32[64,2,1]{1,2,0:T(1,128)S(1)}, u32[]{:S(2)}, u32[]{:S(2)}) async-start(s32[64,2,1]{1,2,0:T(1,128)} %bitcast.3), calls=%async_computation | async-start | bytes 65536 | tf_op jit(solution)/shard_map/all_to_all | solution.py:59
  350.4 146.2 %all-to-all-start.2 = ((bf16[128,192,256]{0,1,2:T(8,128)(2,1)}), bf16[128,192,256]{0,1,2:T(8,128)(2,1)}, u32[]{:S(2)}, u32[]{:S(2)}) async-start(bf16[128,192,256]{0,1,2:T(8,128)(2,1)} %copy.28), calls=%async_computation.2 | async-start | bytes 25165824 | tf_op jit(solution)/shard_map/all_to_all | solution.py:61
  356.7 146.6 %copy-start = (f32[3072]{0:T(1024)S(1)}, f32[3072]{0:T(1024)}, u32[]{:S(2)}) copy-start(f32[3072]{0:T(1024)} %param.17) | copy-start | bytes 36868
  356.7 146.6 %copy-start.1 = (f32[64]{0:T(128)S(1)}, f32[64]{0:T(128)}, u32[]{:S(2)}) copy-start(f32[64]{0:T(128)} %param.16) | copy-start | bytes 772
where the time goes:
time: 506 us; the launch traced here: 504 us
  waiting for transfers between devices  274 us (54%)
  blocking collectives  137 us (27%)
  local copies, waits for them, and re-layouts  46 us (9%)
  starting transfers between devices  25.4 us (5%)
  matrix products  16.4 us (3%)
    all_to_all x1, waiting for transfers between devices, shards(): lax.all_to_all(outbox, 'blk', split_axis=0, concat_axis=0, tiled=True)  274 us
    all_gather x1, blocking collectives, shards(): all_ids = lax.all_gather(tile_ids, 'rep', axis=0, tiled=True)  137 us
    all_to_all x1, local copies, waits for them, and re-layouts, shards(): lax.all_to_all(outbox, 'blk', split_axis=0, concat_axis=0, tiled=True)  18.1 us
    scatter x1, local copies, waits for them, and re-layouts, shards(): outbox = jnp.zeros((blk_count * capacity, tile_width, row_count), jnp.bfl...  14.9 us
    all_to_all x1, starting transfers between devices, shards(): lax.all_to_all(outbox, 'blk', split_axis=0, concat_axis=0, tiled=True)  13.1 us
  transfers between devices with their start and end apart: 3, of which 1 were waited for; matrix products, arithmetic and copies ran while one was open for 4% of the time, Pallas kernels for 0%

commit v1 on v0

v1 whole, which is shorter than its diff:
```python
import functools

import jax
import jax.numpy as jnp
from jax import lax
from jax.experimental import pallas as pl
from jax.experimental.pallas import tpu as pltpu
from jax.sharding import PartitionSpec as P

MESH = pl.DeviceIdType.MESH
NX, NZ, NC, NY = 4, 8, 2, 4
CELL = 96
CHUNKS = 3
ROWS16 = 16
LANES = 128


def place():
    b = lax.axis_index("blk")
    return b // (NZ * NC), (b // NC) % NZ, b % NC, lax.axis_index("rep")


def device(x, z, c, y):
    return (x * (NZ * NC) + z * NC + c, y)


def greet(peers):
    barrier = pltpu.get_barrier_semaphore()
    for peer in peers:
        pl.semaphore_signal(barrier, inc=1, device_id=peer, device_id_type=MESH)
    pl.semaphore_wait(barrier, len(peers))


def remote(src, dst, send, recv, peer):
    return pltpu.make_async_remote_copy(
        src_ref=src, dst_ref=dst, send_sem=send, recv_sem=recv, device_id=peer, device_id_type=MESH
    )


COLUMN = [(dy, dc) for dy in range(NY) for dc in range(NC) if (dy, dc) != (0, 0)]


def partials_kernel(
    live_ref, enc_ref, amp_ref, keep_ref, panels_hbm, out_ref, table_ref,
    panels_v, amp_v, got, mine, in_sem, s1, r1, s2, r2, s3, r3, groups,
):
    x, z, c, y = place()
    me = y * NC + c
    slots = panels_hbm.shape[0]
    reads = []
    for g, (lo, n) in enumerate(groups):
        cp = pltpu.make_async_copy(panels_hbm.at[pl.ds(lo, n)], panels_v.at[pl.ds(lo, n)], in_sem.at[g])
        cp.start()
        reads.append(cp)
    col = [device(x, z, (c + dc) % NC, (y + dy) % NY) for dy, dc in COLUMN]
    zs = [device(x, (z + d) % NZ, c, y) for d in range(1, NZ)]
    xs = [device((x + d) % NX, z, c, y) for d in range(1, NX)]
    greet(col + zs + xs)
    first = [remote(enc_ref, got.at[me], s1.at[i], r1.at[i], p) for i, p in enumerate(col)]
    for cp in first:
        cp.start()
    got[me] = enc_ref[...]
    amp_v[...] = amp_ref[...] * keep_ref[...]
    lane = lax.broadcasted_iota(jnp.int32, (1, amp_v.shape[1]), 1)
    width = panels_v.shape[1]

    def one(s, carry):
        mask = jnp.where(
            lane < 2 * width,
            jnp.where(lane < width, live_ref[s, 0], live_ref[s, 1]),
            jnp.where(lane < 3 * width, live_ref[s, 2], live_ref[s, 3]),
        ).astype(jnp.bfloat16)
        panel = panels_v[s] * mask
        acc = lax.dot_general(
            amp_v[...], panel, (((1,), (1,)), ((), ())), preferred_element_type=jnp.float32
        )
        low = acc[:, :LANES].reshape(8, 32, LANES)
        high = acc[:, LANES:].reshape(8, 32, width - LANES)
        out_ref[0, :, s] = low[:, :16].astype(jnp.bfloat16)
        out_ref[1, :, s] = low[:, 16:].astype(jnp.bfloat16)
        out_ref[2, :, s] = jnp.concatenate([high[:, :16], high[:, 16:]], axis=-1).astype(jnp.bfloat16)
        return carry

    def work(g):
        reads[g].wait()
        lo, n = groups[g]
        lax.fori_loop(lo, lo + n, one, 0)

    work(0)
    for cp in first:
        cp.wait()
    for i in range(8):
        mine[pl.ds(i, 1), :] = got[i, pl.ds(0, 1), :]
    second = [remote(mine, table_ref.at[x, z], s2.at[i], r2.at[i], p) for i, p in enumerate(zs)]
    for cp in second:
        cp.start()
    table_ref[x, z] = mine[...]
    work(1)
    for cp in second:
        cp.wait()
    third = [remote(table_ref.at[x], table_ref.at[x], s3.at[i], r3.at[i], p) for i, p in enumerate(xs)]
    for cp in third:
        cp.start()
    for g in range(2, len(groups)):
        work(g)
    for cp in third:
        cp.wait()


def partials(live, enc, amplitudes, keep, panels):
    slots, width, kdim = panels.shape
    groups = []
    lo = 0
    while lo < slots:
        n = min(9, slots - lo)
        groups.append((lo, n))
        lo += n
    vmem = pl.BlockSpec(memory_space=pltpu.VMEM)
    return pl.pallas_call(
        functools.partial(partials_kernel, groups=tuple(groups)),
        out_shape=(
            jax.ShapeDtypeStruct((CHUNKS, 8, slots, ROWS16, LANES), jnp.bfloat16),
            jax.ShapeDtypeStruct((NX, NZ, 8, LANES), jnp.int32),
        ),
        in_specs=[pl.BlockSpec(memory_space=pltpu.SMEM), vmem, vmem, vmem, pl.BlockSpec(memory_space=pl.ANY)],
        out_specs=(vmem, vmem),
        scratch_shapes=[
            pltpu.VMEM(panels.shape, jnp.bfloat16),
            pltpu.VMEM(amplitudes.shape, jnp.bfloat16),
            pltpu.VMEM((8, 8, LANES), jnp.int32),
            pltpu.VMEM((8, LANES), jnp.int32),
            pltpu.SemaphoreType.DMA((len(groups),)),
            pltpu.SemaphoreType.DMA((7,)),
            pltpu.SemaphoreType.DMA((7,)),
            pltpu.SemaphoreType.DMA((7,)),
            pltpu.SemaphoreType.DMA((7,)),
            pltpu.SemaphoreType.DMA((3,)),
            pltpu.SemaphoreType.DMA((3,)),
        ],
        compiler_params=pltpu.CompilerParams(
            collective_id=0, has_side_effects=True, vmem_limit_bytes=56 * 1024 * 1024
        ),
    )(live, enc, amplitudes, keep, panels)


def exchange_kernel(
    cell, part_hbm, slot_ref, rank_ref, out_ref,
    yr, pf, pb, smat, sown, tmat, xs_buf, xr_buf, dense, zsp, zrp, zsm, zrm, fx, fr,
    loc_sem, ys, yrs, xs, xrs, zps, zprs, zms, zmrs, cs, crs,
):
    x, z, c, y = place()
    me = y * NC + c
    slots = part_hbm.shape[2]
    total = 8 * slots
    kpad = pb.shape[1]
    col = [(((y + dy) % NY) * NC + (c + dc) % NC, device(x, z, (c + dc) % NC, (y + dy) % NY)) for dy, dc in COLUMN]
    xpeers = [device((x + d) % NX, z, c, y) for d in range(1, NX)]
    up, down = device(x, (z + 1) % NZ, c, y), device(x, (z + NZ - 1) % NZ, c, y)
    partner = device(x, z, (c + 1) % NC, y)
    greet([p for _, p in col] + xpeers + [up, down])

    def y_start(q):
        cps = [remote(part_hbm.at[q, b], yr.at[q, me], ys.at[q, i], yrs.at[q, i], p) for i, (b, p) in enumerate(col)]
        for cp in cps:
            cp.start()
        own = pltpu.make_async_copy(part_hbm.at[q, me], yr.at[q, me], loc_sem.at[q])
        own.start()
        return cps + [own]

    def merge(q):
        def widen(b, carry):
            v = yr[q, b].astype(jnp.float32)
            pf[pl.ds(b * (slots * ROWS16), slots * ROWS16), :] = v.reshape(slots * ROWS16, LANES)
            return carry

        lax.fori_loop(0, 8, widen, 0)

        def rows(i, carry):
            r = 2 * i
            a = pf[pl.ds(r, kpad, stride=ROWS16), :].astype(jnp.bfloat16)
            b = pf[pl.ds(r + 1, kpad, stride=ROWS16), :].astype(jnp.bfloat16)
            p = jnp.concatenate([a, b], axis=1)
            pb[i] = p
            m = jnp.dot(smat[...], p, preferred_element_type=jnp.float32).astype(jnp.bfloat16)
            xs_buf[q, r] = m[:, :LANES]
            xs_buf[q, r + 1] = m[:, LANES:]
            return carry

        lax.fori_loop(0, ROWS16 // 2, rows, 0)

    def x_start(q):
        cps = []
        for i, p in enumerate(xpeers):
            part = pl.ds(i * cell, cell)
            cps.append(remote(xs_buf.at[q, :, part], xr_buf.at[q, :, part], xs.at[q, i], xrs.at[q, i], p))
        for cp in cps:
            cp.start()
        return cps

    def own_part(q):
        def rows(i, carry):
            r = 2 * i
            d = jnp.dot(sown[...], pb[i], preferred_element_type=jnp.float32)
            d = d.reshape(NZ, 32, 2 * LANES)
            dense[q, :, r] = d[:, :, :LANES]
            dense[q, :, r + 1] = d[:, :, LANES:]
            return carry

        lax.fori_loop(0, ROWS16 // 2, rows, 0)

    def gather(q):
        def rows(i, carry):
            r = 2 * i
            p = jnp.concatenate([xr_buf[q, r], xr_buf[q, r + 1]], axis=1)
            d = jnp.dot(tmat[...], p, preferred_element_type=jnp.float32)
            d = d.reshape(NZ, 32, 2 * LANES)
            dense[q, :, r] += d[:, :, :LANES]
            dense[q, :, r + 1] += d[:, :, LANES:]
            return carry

        lax.fori_loop(0, ROWS16 // 2, rows, 0)

    half = ROWS16 // 2

    def z_first(q):
        far = (z + 4) % NZ
        zsp[q, 0, :half] = dense[q, far, :half].astype(jnp.bfloat16)
        zsm[q, 0, half:] = dense[q, far, half:].astype(jnp.bfloat16)
        lo, hi = pl.ds(0, half), pl.ds(half, half)
        a = remote(zsp.at[q, 0, lo], zrp.at[q, 0, lo], zps.at[q, 0], zprs.at[q, 0], up)
        b = remote(zsm.at[q, 0, hi], zrm.at[q, 0, hi], zms.at[q, 0], zmrs.at[q, 0], down)
        a.start()
        b.start()
        return a, b

    def z_step(q, t, before):
        a, b = before
        dp, dm = (z + 4 - t) % NZ, (z + 4 + t) % NZ
        a.wait()
        if t == 1:
            zsp[q, t, :half] = (dense[q, dp, :half] + zrp[q, 0, :half].astype(jnp.float32)).astype(jnp.bfloat16)
            zsp[q, t, half:] = dense[q, dp, half:].astype(jnp.bfloat16)
        else:
            zsp[q, t] = (dense[q, dp] + zrp[q, t - 1].astype(jnp.float32)).astype(jnp.bfloat16)
        a = remote(zsp.at[q, t], zrp.at[q, t], zps.at[q, t], zprs.at[q, t], up)
        a.start()
        b.wait()
        if t == 1:
            zsm[q, t, half:] = (dense[q, dm, half:] + zrm[q, 0, half:].astype(jnp.float32)).astype(jnp.bfloat16)
            zsm[q, t, :half] = dense[q, dm, :half].astype(jnp.bfloat16)
        else:
            zsm[q, t] = (dense[q, dm] + zrm[q, t - 1].astype(jnp.float32)).astype(jnp.bfloat16)
        b = remote(zsm.at[q, t], zrm.at[q, t], zms.at[q, t], zmrs.at[q, t], down)
        b.start()
        return a, b

    def z_last(q, before):
        a, b = before
        a.wait()
        b.wait()
        f = dense[q, z] + zrp[q, 3].astype(jnp.float32) + zrm[q, 3].astype(jnp.float32)
        fx[q, 0] = f[:, :16]
        fx[q, 1] = f[:, 16:]
        cp = remote(fx.at[q, 1 - c], fr.at[q], cs.at[q], crs.at[q], partner)
        cp.start()
        return cp

    def z_all(q):
        st = z_first(q)
        for t in range(1, 4):
            st = z_step(q, t, st)
        return z_last(q, st)

    ycp = y_start(0)
    iota = lax.broadcasted_iota(jnp.int32, (cell, kpad), 0)
    for i in range(3):
        smat[pl.ds(i * cell, cell), :] = (slot_ref[pl.ds(i, 1), :kpad] == iota).astype(jnp.bfloat16)
    iota = lax.broadcasted_iota(jnp.int32, (NZ * 32, kpad), 0)
    sown[...] = (slot_ref[pl.ds(3, 1), :kpad] == iota).astype(jnp.bfloat16)
    iota = lax.broadcasted_iota(jnp.int32, (NZ * 32, 3 * cell), 1)
    hit = rank_ref[:, 0:1] == iota
    for i in range(1, 3):
        hit = hit | ((rank_ref[:, i : i + 1] >= 0) & (rank_ref[:, i : i + 1] + i * cell == iota))
    tmat[...] = hit.astype(jnp.bfloat16)
    pf[pl.ds(total * ROWS16, (kpad - total) * ROWS16), :] = jnp.zeros(((kpad - total) * ROWS16, LANES), jnp.float32)

    xcp = {}
    last = {}
    for q in range(CHUNKS):
        for cp in ycp:
            cp.wait()
        if q + 1 < CHUNKS:
            ycp = y_start(q + 1)
        merge(q)
        xcp[q] = x_start(q)
        own_part(q)
        if q >= 1:
            for cp in xcp[q - 1]:
                cp.wait()
            gather(q - 1)
            last[q - 1] = z_all(q - 1)
    q = CHUNKS - 1
    for cp in xcp[q]:
        cp.wait()
    gather(q)
    last[q] = z_all(q)
    for q in range(CHUNKS):
        last[q].wait()
        out_ref[q, c] = fx[q, c]
        out_ref[q, 1 - c] = fr[q]


def exchange(cell, ident, part, slot, rank):
    slots = part.shape[2]
    kpad = (8 * slots + 15) // 16 * 16
    vmem = pl.BlockSpec(memory_space=pltpu.VMEM)
    dma = pltpu.SemaphoreType.DMA
    bf, f32 = jnp.bfloat16, jnp.float32
    zbuf = pltpu.VMEM((CHUNKS, 4, ROWS16, 32, LANES), bf)
    return pl.pallas_call(
        functools.partial(exchange_kernel, cell),
        out_shape=jax.ShapeDtypeStruct((CHUNKS, NC, ROWS16, 16, LANES), f32),
        in_specs=[pl.BlockSpec(memory_space=pl.ANY), vmem, vmem],
        out_specs=vmem,
        scratch_shapes=[
            pltpu.VMEM((CHUNKS, 8, slots, ROWS16, LANES), bf),
            pltpu.VMEM((kpad * ROWS16, LANES), f32),
            pltpu.VMEM((ROWS16 // 2, kpad, 2 * LANES), bf),
            pltpu.VMEM((3 * cell, kpad), bf),
            pltpu.VMEM((NZ * 32, kpad), bf),
            pltpu.VMEM((NZ * 32, 3 * cell), bf),
            pltpu.VMEM((CHUNKS, ROWS16, 3 * cell, LANES), bf),
            pltpu.VMEM((CHUNKS, ROWS16, 3 * cell, LANES), bf),
            pltpu.VMEM((CHUNKS, NZ, ROWS16, 32, LANES), f32),
            zbuf, zbuf, zbuf, zbuf,
            pltpu.VMEM((CHUNKS, NC, ROWS16, 16, LANES), f32),
            pltpu.VMEM((CHUNKS, ROWS16, 16, LANES), f32),
            dma((CHUNKS,)),
            dma((CHUNKS, 7)), dma((CHUNKS, 7)),
            dma((CHUNKS, 3)), dma((CHUNKS, 3)),
            dma((CHUNKS, 4)), dma((CHUNKS, 4)),
            dma((CHUNKS, 4)), dma((CHUNKS, 4)),
            dma((CHUNKS,)), dma((CHUNKS,)),
        ],
        compiler_params=pltpu.CompilerParams(
            collective_id=ident, has_side_effects=True, vmem_limit_bytes=60 * 1024 * 1024
        ),
    )(part, slot, rank)


def finish_kernel(g_ref, occ_ref, vir_ref, keep_ref, out_ref):
    def tile(t):
        blocks = []
        for c in range(NC):
            part = [g_ref[pl.ds((q * NC + c) * 256 + t, 16, stride=16), :] for q in range(CHUNKS)]
            low = jnp.concatenate(part[:2], axis=0)
            high = jnp.concatenate([part[2][:, :64], part[2][:, 64:]], axis=0)
            blocks.append(jnp.concatenate([low, high], axis=1))
        return jnp.concatenate(blocks, axis=0)

    occ = occ_ref[...]
    for t in range(8):
        pair = jnp.concatenate([tile(2 * t), tile(2 * t + 1)], axis=1)
        cols = pl.ds(t * 384, 384)
        ratio = pair / (occ - vir_ref[:, cols])
        out_ref[:, cols] = jnp.where(keep_ref[:, cols] > 0, ratio, 0.0).astype(jnp.bfloat16)


def finish(g, occ, vir, keep):
    return pl.pallas_call(
        finish_kernel,
        out_shape=jax.ShapeDtypeStruct((occ.shape[0], vir.shape[1]), jnp.bfloat16),
    )(g.reshape(CHUNKS * NC * ROWS16 * 16, LANES), occ, vir, keep)


def shards(
    amplitudes,
    panels,
    panel_owner_index,
    panel_target_tile,
    panel_tile_mask,
    tile_sizes,
    tile_irreps,
    occ_energy,
    vir_energy,
):
    x, z, c, y = place()
    blk_index = lax.axis_index("blk")
    dev = blk_index * NY + y
    slots, width, kdim = panels.shape
    tiles_here = kdim // width
    owned = 16
    in_tile = jnp.arange(width, dtype=jnp.int32)
    sizes_here = lax.dynamic_slice_in_dim(tile_sizes, dev * tiles_here, tiles_here, 0)
    keep_cols = (in_tile[None, :] < sizes_here[:, None]).reshape(1, kdim).astype(jnp.bfloat16)
    target = panel_owner_index[:, 0] * owned + panel_target_tile
    irrep_source = lax.dynamic_slice_in_dim(tile_irreps, dev * tiles_here, tiles_here, 0)
    irrep_target = tile_irreps[target]
    live = panel_tile_mask * (irrep_source[None, :] == irrep_target[:, None]).astype(jnp.int32)
    enc = jnp.where(jnp.max(live, axis=1) > 0, target, -1)
    enc = jnp.broadcast_to(jnp.pad(enc, (0, LANES - slots), constant_values=-1)[None, :], (8, LANES))
    part, table = partials(live.astype(jnp.float32), enc, amplitudes, keep_cols, panels)

    ids = table[..., :slots].reshape(NX * NZ, 8 * slots)
    group = jnp.arange(32, dtype=jnp.int32)
    hi = ((ids[..., None] >> 5) == group).astype(jnp.bfloat16)
    lo = ((ids[..., None] & 31) == group).astype(jnp.bfloat16)
    named = jnp.einsum("csh,csl->chl", hi, lo, preferred_element_type=jnp.float32) > 0
    named = named.reshape(NX, NZ, NX, NZ * 32)
    load = jnp.sum(named.astype(jnp.int32), axis=-1)
    across = jnp.arange(NX)[:, None, None] != jnp.arange(NX)[None, None, :]
    most = jnp.max(jnp.where(across, load, 0))
    plane = lax.dynamic_index_in_dim(named, z, 1, keepdims=False)
    dist = jnp.arange(1, NX)
    mine = lax.dynamic_index_in_dim(ids.reshape(NX, NZ, 8 * slots)[:, :, :], z, 1, keepdims=False)
    mine = lax.dynamic_index_in_dim(mine, x, 0, keepdims=False)
    ahead = (x + dist) % NX
    behind = (x - dist) % NX
    sends = plane[x][ahead]
    takes = plane[behind, x]
    both = jnp.concatenate([sends, takes], axis=0)
    spot = jnp.arange(NZ * 32)
    before = (spot[:, None] < spot[None, :]).astype(jnp.bfloat16)
    rank = jnp.dot(both.astype(jnp.bfloat16), before, preferred_element_type=jnp.float32).astype(jnp.int32)
    rank = jnp.where(both, rank, -1)
    rel = mine[None, :] - ahead[:, None] * (NZ * 32)
    slot = jnp.max(jnp.where(rel[:, None, :] == spot[None, :, None], rank[:3, :, None], -1), axis=1)
    own = jnp.where((mine >= x * 256) & (mine < x * 256 + 256), mine - x * 256, -1)
    slot = jnp.concatenate([slot, own[None, :]], axis=0)
    slot = jnp.pad(slot, ((0, 4), (0, 384 - 8 * slots)), constant_values=-1)
    rank_cols = jnp.pad(rank[3:].T, ((0, 0), (0, LANES - 3)), constant_values=-1)

    summed = lax.cond(
        most <= CELL,
        functools.partial(exchange, CELL, 1),
        functools.partial(exchange, NZ * 32, 2),
        part, slot, rank_cols,
    )
    sizes_owned = lax.dynamic_slice_in_dim(tile_sizes, blk_index * owned, owned, 0)
    keep_out = (in_tile[None, :] < sizes_owned[:, None]).astype(jnp.float32).reshape(1, owned * width)
    return finish(summed, occ_energy[:, None], vir_energy[None, :], keep_out)


def solution(mesh):
    return jax.shard_map(
        shards,
        mesh=mesh,
        in_specs=(
            P(None, ("blk", "rep")),
            P(("blk", "rep"), None, None),
            P(("blk", "rep"), None),
            P(("blk", "rep")),
            P(("blk", "rep"), None),
            P(),
            P(),
            P("rep"),
            P("blk"),
        ),
        out_specs=P("rep", "blk"),
        check_vma=False,
    )
```

time: 506 us -> 161 us (0.32)
  waiting for transfers between devices: 274 us -> 0 us
  Pallas kernels: 0 us -> 142 us
  blocking collectives: 137 us -> 0 us
  local copies, waits for them, and re-layouts: 46 us -> 10.8 us
  starting transfers between devices: 25.4 us -> 0 us
  matrix products: 16.4 us -> 0.84 us
    all_to_all x3 -> x0, waiting for transfers between devices: 274 us -> none  [the longest x1 274 us: shards(): lax.all_to_all(outbox, 'blk', split_axis=0, concat_axis=0, tiled=True)]
    pallas_call x0 -> x3, Pallas kernels: none -> 142 us  [the longest x1 110 us: exchange(): pl.pallas_call(functools.partial(exchange_kernel, cell), out_shape=jax.Sh...]
    all_gather x1 -> x0, blocking collectives: 137 us -> none  [shards(): all_ids = lax.all_gather(tile_ids, 'rep', axis=0, tiled=True)]
    all_to_all x3 -> x0, starting transfers between devices: 25.4 us -> none  [the longest x1 13.1 us: shards(): lax.all_to_all(outbox, 'blk', split_axis=0, concat_axis=0, tiled=True)]
    all_to_all x3 -> x0, local copies, waits for them, and re-layouts: 19.4 us -> none  [the longest x1 18.1 us: shards(): lax.all_to_all(outbox, 'blk', split_axis=0, concat_axis=0, tiled=True)]
    scatter x2 -> x0, local copies, waits for them, and re-layouts: 15.8 us -> none  [the longest x1 14.9 us: shards(): outbox = jnp.zeros((blk_count * capacity, tile_width, row_count), jnp.bfl...]
    dot_general x2, matrix products: 16.4 us -> 0.84 us  [the longest x1 0.68 us: shards(): jnp.einsum('csh,csl->chl', hi, lo, preferred_element_type=jnp.float32) > 0]
  transfers between devices with their start and end apart: 3 -> 0, of which waited for: 1 -> 0; matrix products, arithmetic and copies ran while one was open for 4% -> 0% of each run, Pallas kernels for 0% -> 0%
where the time goes in v1:
time: 161 us; the launch traced here: 160 us
  Pallas kernels  142 us (88%)
  local copies, waits for them, and re-layouts  10.8 us (7%)
  other arithmetic  5.34 us (3%)
    pallas_call x1, Pallas kernels, exchange(): pl.pallas_call(functools.partial(exchange_kernel, cell), out_shape=jax.Sh...  110 us
    pallas_call x1, Pallas kernels, partials(): pl.pallas_call(functools.partial(partials_kernel, groups=tuple(groups)),...  29.9 us

profile of v1, /device:TPU:1, one launch (start us, length us, event | category | flops | bytes accessed | tf_op | source)
XLA Modules:
  0.0 160.4 jit_solution(2923183168488838493)
XLA Ops:
  0.0 0.8 dynamic_slice.22
  0.8 0.8 copy.24
  1.5 0.7 compare_select_fusion.3
  2.2 1.5 gather_fusion
  3.7 0.8 fusion.9
  4.5 0.7 compare_select_fusion.10
  5.2 0.6 broadcast_in_dim.47.enc_ref
  5.8 0.8 dynamic_slice.23
  6.6 0.7 reshape.281.keep_ref
  7.3 29.9 %shard_map.91 = (bf16[3,8,43,16,128]{4,3,2,1,0:T(8,128)(2,1)}, s32[4,8,8,128]{3,2,1,0:T(8,128)}) custom-call(f32[43,4]{1,0:T(8,128)} %get-tuple-element.85.live_ref, s32[8,128]{1,0:T(8,128)} %broadcast_in_dim.47.enc_ref, bf16[256,768]{1,0:T(8,128)(2,1)} %amp_ref.1, bf16[1,768]{1,0:T(2,128)(2,1)} %reshape.281.keep_ref, bf16[43,192,768]{2,1,0:T(8,128)(2,1)} %panels_hbm.1), custom_call_target="tpu_custom_call" | custom-call | tf_op jit(solution)/shard_map/pallas_call | solution.py:119
  37.2 0.9 fusion.28
  38.2 0.1 shift_right_arithmetic.16
  38.3 0.7 fusion.5
  39.0 0.1 and_convert_fusion
  39.1 0.3 copy.26
  39.4 0.2 reshape.280
  39.7 0.6 gather_fusion.1
  40.3 0.6 gather_fusion.2
  40.9 0.2 fusion.6
  41.3 0.4 select_reduce_fusion
  41.7 0.1 convert_reduce_fusion
  42.0 0.6 reduce_sum.18
  42.7 0.7 select_reduce_fusion.1
  44.1 112.1 %conditional.1 = (f32[1536,128]{1,0:T(8,128)S(1)}) conditional(s32[]{:T(128)} %convert_element_type.40, (s32[4,344]{1,0:T(4,128)S(1)}, s32[256,3]{0,1:T(4,128)S(1)}, bf16[3,8,43,16,128]{4,3,2,1,0:T(8,128)(2,1)}) %tuple.17, (s32[4,344]{1,0:T(4,128)S(1)}, s32[256,3]{0,1:T(4,128)S(1)}, bf16[3,8,43,16,128]{4,3,2,1,0:T(8,128)(2,1)}) %tuple.17), branch_computations={%region_5.6_spmd, %region_6.7_spmd} | conditional | bytes 158096 | solution.py:433
  44.3 0.1 copy.28
  44.4 0.7 pad.23.rank_ref
  45.1 0.6 pad.22.slot_ref
  45.7 110.5 %branch_1_fun.2 = f32[3,2,16,16,128]{4,3,2,1,0:T(8,128)S(1)} custom-call(bf16[3,8,43,16,128]{4,3,2,1,0:T(8,128)(2,1)} %get-tuple-element.48.part_hbm, s32[8,384]{1,0:T(8,128)} %pad.22.slot_ref, s32[256,128]{1,0:T(8,128)} %pad.23.rank_ref), custom_call_target="tpu_custom_call" | custom-call | tf_op jit(solution)/shard_map/cond/branch_1_fun/pallas_call | solution.py:320
  156.2 0.8 dynamic_slice.27
  157.0 0.7 reshape.282.keep_ref
  157.7 0.7 copy.29.occ_ref
  158.4 1.9 %shard_map.92 = bf16[64,3072]{1,0:T(8,128)(2,1)} custom-call(f32[1536,128]{1,0:T(8,128)S(1)} %get-tuple-element.90.g_ref, f32[64,1]{1,0:T(8,128)} %copy.29.occ_ref, f32[1,3072]{1,0:T(1,128)} %bitcast.30, f32[1,3072]{1,0:T(1,128)} %reshape.282.keep_ref), custom_call_target="tpu_custom_call" | custom-call | tf_op jit(solution)/shard_map/pallas_call | solution.py:370
  (20 shorter events, 0.7 us)
Async XLA Ops:
  44.0 113.7 %copy-start = (f32[64]{0:T(128)S(1)}, f32[64]{0:T(128)}, u32[]{:S(2)}) copy-start(f32[64]{0:T(128)} %param.18) | copy-start | bytes 772

commit v2 on v0

v2 whole, which is shorter than its diff:
```python
import functools

import jax
import jax.numpy as jnp
from jax import lax
from jax.experimental import pallas as pl
from jax.experimental.pallas import tpu as pltpu
from jax.sharding import PartitionSpec as P

MESH = pl.DeviceIdType.MESH
NX, NZ, NC, NY = 4, 8, 2, 4
CELL = 96
CHUNKS = 3
R = 16
LANES = 128
SEG = 48
KPAD = 8 * SEG
OWNED = 16
SPOTS = NZ * NC * OWNED
ZT = NC * OWNED
COLUMN = [(dy, dc) for dy in range(NY) for dc in range(NC) if (dy, dc) != (0, 0)]


def place():
    b = lax.axis_index("blk")
    return b // (NZ * NC), (b // NC) % NZ, b % NC, lax.axis_index("rep")


def device(x, z, c, y):
    return (x * (NZ * NC) + z * NC + c, y)


def remote(src, dst, send, recv, peer):
    return pltpu.make_async_remote_copy(
        src_ref=src, dst_ref=dst, send_sem=send, recv_sem=recv, device_id=peer, device_id_type=MESH
    )


def start(copies):
    for cp in copies:
        cp.start()
    return copies


def wait(copies):
    for cp in copies:
        cp.wait()


def ladder_kernel(
    cell, groups,
    owner_ref, target_ref, mask_ref, sizes_ref, irreps_ref, amp_ref, panels_hbm, out_ref, most_ref,
    panels_v, amp_v, part, yr, pf, pb, smat, sown, tmat, xsend, xrecv, dense,
    zsp, zrp, zsm, zrm, fx, fr, enc, got, mine, xids, cnt, zcnt, xcnt,
    in_sem, own_sem, ys, yr_sem, xs, xr_sem, zps, zpr, zms, zmr, cs, cr,
    is_, ir, jsend, jrecv, ks, kr, ls, lr,
):
    x, z, c, y = place()
    me = y * NC + c
    dev = lax.axis_index("blk") * NY + y
    slots, width, kdim = panels_v.shape
    tiles = kdim // width
    reads = start([
        pltpu.make_async_copy(panels_hbm.at[pl.ds(lo, n)], panels_v.at[pl.ds(lo, n)], in_sem.at[g])
        for g, (lo, n) in enumerate(groups)
    ])
    col = [(((y + dy) % NY) * NC + (c + dc) % NC, device(x, z, (c + dc) % NC, (y + dy) % NY)) for dy, dc in COLUMN]
    xpeers = [device((x + d) % NX, z, c, y) for d in range(1, NX)]
    zpeers = [device(x, (z + d) % NZ, c, y) for d in range(1, NZ)]
    up, down = zpeers[0], zpeers[NZ - 2]
    partner = device(x, z, (c + 1) % NC, y)
    barrier = pltpu.get_barrier_semaphore()
    peers = [p for _, p in col] + xpeers + zpeers
    for p in peers:
        pl.semaphore_signal(barrier, inc=1, device_id=p, device_id_type=MESH)

    sources = [irreps_ref[dev * tiles + j] for j in range(tiles)]

    def target_of(s):
        return owner_ref[s, 0] * OWNED + target_ref[s]

    def live_of(s):
        kind = irreps_ref[target_of(s)]
        return [jnp.where(kind == sources[j], mask_ref[s, j], 0) for j in range(tiles)]

    seg_lane = lax.broadcasted_iota(jnp.int32, (8, KPAD), 1)

    def encode(s, row):
        live = live_of(s)
        value = jnp.where(live[0] + live[1] + live[2] + live[3] > 0, target_of(s) + 1, 0)
        return jnp.where(seg_lane == me * SEG + s, value, row)

    enc[...] = lax.fori_loop(0, slots, encode, jnp.zeros((8, KPAD), jnp.int32))
    lane = lax.broadcasted_iota(jnp.int32, (1, kdim), 1)

    def by_tile(vals):
        v = vals[tiles - 1]
        for j in range(tiles - 2, -1, -1):
            v = jnp.where(lane < (j + 1) * width, vals[j], v)
        return v

    ends = by_tile([sizes_ref[dev * tiles + j] + j * width for j in range(tiles)])
    amp_v[...] = amp_ref[...] * (lane < ends).astype(jnp.bfloat16)
    pl.semaphore_wait(barrier, len(peers))
    icp = start([remote(enc, got.at[me], is_.at[i], ir.at[i], p) for i, (b, p) in enumerate(col)])
    got[me] = enc[...]

    def one(s, carry):
        mask = by_tile(live_of(s)).astype(jnp.bfloat16)
        acc = lax.dot_general(
            amp_v[...], panels_v[s] * mask, (((1,), (1,)), ((), ())), preferred_element_type=jnp.float32
        )
        low = acc[:, :LANES].reshape(8, 2 * R, LANES)
        high = acc[:, LANES:].reshape(8, 2 * R, width - LANES)
        part[0, :, s] = low[:, :R].astype(jnp.bfloat16)
        part[1, :, s] = low[:, R:].astype(jnp.bfloat16)
        part[2, :, s] = jnp.concatenate([high[:, :R], high[:, R:]], axis=-1).astype(jnp.bfloat16)
        return carry

    def y_start(q, g):
        lo, n = groups[g] if g is not None else (0, slots)
        k = g if g is not None else 0
        return start([
            remote(part.at[q, b, pl.ds(lo, n)], yr.at[q, me, pl.ds(lo, n)], ys.at[q, k, i], yr_sem.at[q, k, i], p)
            for i, (b, p) in enumerate(col)
        ])

    ycp = {0: []}
    for g, (lo, n) in enumerate(groups):
        reads[g].wait()
        lax.fori_loop(lo, lo + n, one, 0)
        ycp[0] += y_start(0, g)
    ycp[1] = y_start(1, None)
    own = start([pltpu.make_async_copy(part.at[q, me], yr.at[q, me], own_sem.at[q]) for q in range(CHUNKS)])

    wait(icp)
    row = got[0]
    for b in range(1, 8):
        row = row + got[b]
    mine[...] = row
    jcp = start([remote(mine, xids.at[i], jsend.at[i], jrecv.at[i], p) for i, p in enumerate(xpeers)])
    spot = lax.broadcasted_iota(jnp.int32, (SPOTS, KPAD), 0)
    lower = (
        lax.broadcasted_iota(jnp.int32, (SPOTS, SPOTS), 0) >= lax.broadcasted_iota(jnp.int32, (SPOTS, SPOTS), 1)
    ).astype(jnp.bfloat16)

    def ranks(ids, group):
        hit = ids - (group * SPOTS + 1) == spot
        named = jnp.max(hit.astype(jnp.float32), axis=1, keepdims=True)
        wide = jnp.broadcast_to(named, (SPOTS, LANES))
        rank = jnp.dot(lower, wide.astype(jnp.bfloat16), preferred_element_type=jnp.float32)
        return hit, rank * wide

    count = jnp.zeros((1, LANES), jnp.float32)
    for i in range(NX - 1):
        hit, rank = ranks(mine[0:1, :], (x + i + 1) % NX)
        slot = jnp.sum(jnp.where(hit, rank[:, 0:1], 0.0), axis=0, keepdims=True)
        nth = (lax.broadcasted_iota(jnp.int32, (cell, KPAD), 0) + 1).astype(jnp.float32)
        smat[pl.ds(i * cell, cell), :] = (slot == nth).astype(jnp.bfloat16)
        count = jnp.maximum(count, jnp.max(rank, axis=0, keepdims=True))
    sown[...] = (mine[0:1, :] - (x * SPOTS + 1) == spot).astype(jnp.bfloat16)
    cnt[...] = jnp.broadcast_to(count, (8, LANES))
    kcp = start([remote(cnt, zcnt.at[z], ks.at[i], kr.at[i], p) for i, p in enumerate(zpeers)])
    zcnt[z] = cnt[...]
    pf[...] = jnp.zeros(pf.shape, jnp.float32)

    def merge(q):
        def widen(b, carry):
            v = yr[q, b].astype(jnp.float32)
            pf[pl.ds(b * (SEG * R), slots * R), :] = v.reshape(slots * R, LANES)
            return carry

        lax.fori_loop(0, 8, widen, 0)

        def rows(i, carry):
            r = 2 * i
            a = pf[pl.ds(r, KPAD, stride=R), :].astype(jnp.bfloat16)
            b = pf[pl.ds(r + 1, KPAD, stride=R), :].astype(jnp.bfloat16)
            p = jnp.concatenate([a, b], axis=1)
            pb[i] = p
            m = jnp.dot(smat[...], p, preferred_element_type=jnp.float32).astype(jnp.bfloat16)
            xsend[q, r] = m[:, :LANES]
            xsend[q, r + 1] = m[:, LANES:]
            return carry

        lax.fori_loop(0, R // 2, rows, 0)

    def x_start(q):
        out = []
        for i, p in enumerate(xpeers):
            cols = pl.ds(i * cell, cell)
            out.append(remote(xsend.at[q, :, cols], xrecv.at[q, :, cols], xs.at[q, i], xr_sem.at[q, i], p))
        return start(out)

    def own_part(q):
        def rows(i, carry):
            r = 2 * i
            d = jnp.dot(sown[...], pb[i], preferred_element_type=jnp.float32).reshape(NZ, ZT, 2 * LANES)
            dense[q, :, r] = d[:, :, :LANES]
            dense[q, :, r + 1] = d[:, :, LANES:]
            return carry

        lax.fori_loop(0, R // 2, rows, 0)

    def gather(q):
        def rows(i, carry):
            r = 2 * i
            p = jnp.concatenate([xrecv[q, r], xrecv[q, r + 1]], axis=1)
            d = jnp.zeros((SPOTS, 2 * LANES), jnp.float32)
            for k in range(NX - 1):
                d += jnp.dot(tmat[k], p[k * cell : (k + 1) * cell], preferred_element_type=jnp.float32)
            d = d.reshape(NZ, ZT, 2 * LANES)
            dense[q, :, r] += d[:, :, :LANES]
            dense[q, :, r + 1] += d[:, :, LANES:]
            return carry

        lax.fori_loop(0, R // 2, rows, 0)

    half = R // 2

    def z_first(q):
        far = (z + 4) % NZ
        zsp[q, 0, :half] = dense[q, far, :half].astype(jnp.bfloat16)
        zsm[q, 0, half:] = dense[q, far, half:].astype(jnp.bfloat16)
        lo, hi = pl.ds(0, half), pl.ds(half, half)
        a = remote(zsp.at[q, 0, lo], zrp.at[q, 0, lo], zps.at[q, 0], zpr.at[q, 0], up)
        b = remote(zsm.at[q, 0, hi], zrm.at[q, 0, hi], zms.at[q, 0], zmr.at[q, 0], down)
        start([a, b])
        return a, b

    def z_step(q, t, before):
        a, b = before
        dp, dm = (z + 4 - t) % NZ, (z + 4 + t) % NZ
        a.wait()
        if t == 1:
            zsp[q, t, :half] = (dense[q, dp, :half] + zrp[q, 0, :half].astype(jnp.float32)).astype(jnp.bfloat16)
            zsp[q, t, half:] = dense[q, dp, half:].astype(jnp.bfloat16)
        else:
            zsp[q, t] = (dense[q, dp] + zrp[q, t - 1].astype(jnp.float32)).astype(jnp.bfloat16)
        a = remote(zsp.at[q, t], zrp.at[q, t], zps.at[q, t], zpr.at[q, t], up)
        a.start()
        b.wait()
        if t == 1:
            zsm[q, t, half:] = (dense[q, dm, half:] + zrm[q, 0, half:].astype(jnp.float32)).astype(jnp.bfloat16)
            zsm[q, t, :half] = dense[q, dm, :half].astype(jnp.bfloat16)
        else:
            zsm[q, t] = (dense[q, dm] + zrm[q, t - 1].astype(jnp.float32)).astype(jnp.bfloat16)
        b = remote(zsm.at[q, t], zrm.at[q, t], zms.at[q, t], zmr.at[q, t], down)
        b.start()
        return a, b

    def z_last(q, before):
        wait(before)
        f = dense[q, z] + zrp[q, 3].astype(jnp.float32) + zrm[q, 3].astype(jnp.float32)
        fx[q, 0] = f[:, :OWNED]
        fx[q, 1] = f[:, OWNED:]
        cp = remote(fx.at[q, 1 - c], fr.at[q], cs.at[q], cr.at[q], partner)
        cp.start()
        return cp

    def z_all(q):
        st = z_first(q)
        for t in range(1, 4):
            st = z_step(q, t, st)
        return z_last(q, st)

    xcp, last = {}, {}
    for q in range(CHUNKS):
        wait(ycp[q])
        own[q].wait()
        if q + 2 < CHUNKS:
            ycp[q + 2] = y_start(q + 2, None)
        merge(q)
        xcp[q] = x_start(q)
        own_part(q)
        if q == 0:
            wait(jcp)
            nth = (lax.broadcasted_iota(jnp.int32, (SPOTS, cell), 1) + 1).astype(jnp.float32)
            for i in range(NX - 1):
                _, rank = ranks(xids[i, 0:1, :], x)
                tmat[i] = (rank[:, 0:1] == nth).astype(jnp.bfloat16)
            wait(kcp)
            cnt[...] = jnp.max(zcnt[...], axis=0)
            lcp = start([remote(cnt, xcnt.at[x], ls.at[i], lr.at[i], p) for i, p in enumerate(xpeers)])
            xcnt[x] = cnt[...]
        if q >= 1:
            wait(xcp[q - 1])
            gather(q - 1)
            last[q - 1] = z_all(q - 1)
    q = CHUNKS - 1
    wait(lcp)
    most_ref[...] = jnp.max(xcnt[...], axis=0)
    wait(xcp[q])
    gather(q)
    last[q] = z_all(q)
    for q in range(CHUNKS):
        last[q].wait()
        out_ref[q, c] = fx[q, c]
        out_ref[q, 1 - c] = fr[q]


def ladder(cell, ident, owner, target, mask, sizes, irreps, amplitudes, panels):
    slots = panels.shape[0]
    groups, lo = [], 0
    while lo < slots:
        n = min(11, slots - lo)
        groups.append((lo, n))
        lo += n
    ng = len(groups)
    vmem = pl.BlockSpec(memory_space=pltpu.VMEM)
    smem = pl.BlockSpec(memory_space=pltpu.SMEM)
    dma = pltpu.SemaphoreType.DMA
    bf, f32, i32 = jnp.bfloat16, jnp.float32, jnp.int32
    zbuf = pltpu.VMEM((CHUNKS, 4, R, ZT, LANES), bf)
    return pl.pallas_call(
        functools.partial(ladder_kernel, cell, tuple(groups)),
        out_shape=(
            jax.ShapeDtypeStruct((CHUNKS, NC, R, OWNED, LANES), f32),
            jax.ShapeDtypeStruct((8, LANES), f32),
        ),
        in_specs=[smem] * 5 + [vmem, pl.BlockSpec(memory_space=pl.ANY)],
        out_specs=(vmem, vmem),
        scratch_shapes=[
            pltpu.VMEM(panels.shape, bf),
            pltpu.VMEM(amplitudes.shape, bf),
            pltpu.VMEM((CHUNKS, 8, slots, R, LANES), bf),
            pltpu.VMEM((CHUNKS, 8, slots, R, LANES), bf),
            pltpu.VMEM((KPAD * R, LANES), f32),
            pltpu.VMEM((R // 2, KPAD, 2 * LANES), bf),
            pltpu.VMEM((3 * cell, KPAD), bf),
            pltpu.VMEM((SPOTS, KPAD), bf),
            pltpu.VMEM((NX - 1, SPOTS, cell), bf),
            pltpu.VMEM((CHUNKS, R, 3 * cell, LANES), bf),
            pltpu.VMEM((CHUNKS, R, 3 * cell, LANES), bf),
            pltpu.VMEM((CHUNKS, NZ, R, ZT, LANES), f32),
            zbuf, zbuf, zbuf, zbuf,
            pltpu.VMEM((CHUNKS, NC, R, OWNED, LANES), f32),
            pltpu.VMEM((CHUNKS, R, OWNED, LANES), f32),
            pltpu.VMEM((8, KPAD), i32),
            pltpu.VMEM((8, 8, KPAD), i32),
            pltpu.VMEM((8, KPAD), i32),
            pltpu.VMEM((NX - 1, 8, KPAD), i32),
            pltpu.VMEM((8, LANES), f32),
            pltpu.VMEM((NZ, 8, LANES), f32),
            pltpu.VMEM((NX, 8, LANES), f32),
            dma((ng,)), dma((CHUNKS,)),
            dma((CHUNKS, ng, 7)), dma((CHUNKS, ng, 7)),
            dma((CHUNKS, 3)), dma((CHUNKS, 3)),
            dma((CHUNKS, 4)), dma((CHUNKS, 4)),
            dma((CHUNKS, 4)), dma((CHUNKS, 4)),
            dma((CHUNKS,)), dma((CHUNKS,)),
            dma((7,)), dma((7,)),
            dma((3,)), dma((3,)),
            dma((7,)), dma((7,)),
            dma((3,)), dma((3,)),
        ],
        compiler_params=pltpu.CompilerParams(
            collective_id=ident, has_side_effects=True, vmem_limit_bytes=62 * 1024 * 1024
        ),
    )(owner, target, mask, sizes, irreps, amplitudes, panels)


def finish_kernel(sizes_ref, g_ref, occ_ref, vir_ref, out_ref):
    rows, cols_all = out_ref.shape
    first = lax.axis_index("blk") * OWNED
    wide = 2 * cols_all // OWNED
    lane = lax.broadcasted_iota(jnp.int32, (1, wide), 1)
    square = lax.broadcasted_iota(jnp.int32, (rows, rows), 0) == lax.broadcasted_iota(jnp.int32, (rows, rows), 1)
    occ = jnp.sum(jnp.where(square, occ_ref[...], 0.0), axis=1, keepdims=True)

    def tile(t):
        blocks = []
        for c in range(NC):
            piece = [g_ref[pl.ds((q * NC + c) * R * OWNED + t, R, stride=OWNED), :] for q in range(CHUNKS)]
            low = jnp.concatenate(piece[:2], axis=0)
            high = jnp.concatenate([piece[2][:, : LANES // 2], piece[2][:, LANES // 2 :]], axis=0)
            blocks.append(jnp.concatenate([low, high], axis=1))
        return jnp.concatenate(blocks, axis=0)

    for t in range(0, OWNED, 2):
        pair = jnp.concatenate([tile(t), tile(t + 1)], axis=1)
        cols = pl.ds(t * wide // 2, wide)
        ends = jnp.where(lane < wide // 2, sizes_ref[first + t], sizes_ref[first + t + 1] + wide // 2)
        ratio = pair / (occ - vir_ref[:, cols])
        out_ref[:, cols] = jnp.where(lane < ends, ratio, 0.0).astype(jnp.bfloat16)


def finish(sizes, g, occ, vir):
    vmem = pl.BlockSpec(memory_space=pltpu.VMEM)
    return pl.pallas_call(
        finish_kernel,
        out_shape=jax.ShapeDtypeStruct((occ.shape[1], vir.shape[1]), jnp.bfloat16),
        in_specs=[pl.BlockSpec(memory_space=pltpu.SMEM), vmem, vmem, vmem],
        out_specs=vmem,
    )(sizes, g.reshape(CHUNKS * NC * R * OWNED, LANES), occ, vir)


def shards(
    amplitudes,
    panels,
    panel_owner_index,
    panel_target_tile,
    panel_tile_mask,
    tile_sizes,
    tile_irreps,
    occ_energy,
    vir_energy,
):
    args = (panel_owner_index, panel_target_tile, panel_tile_mask, tile_sizes, tile_irreps, amplitudes, panels)
    summed, most = ladder(CELL, 0, *args)
    summed = lax.cond(
        most[0, 0] <= CELL,
        lambda first, *rest: first,
        lambda first, *rest: ladder(SPOTS, 1, *rest)[0],
        summed, *args,
    )
    return finish(tile_sizes, summed, occ_energy[None, :], vir_energy[None, :])


def solution(mesh):
    return jax.shard_map(
        shards,
        mesh=mesh,
        in_specs=(
            P(None, ("blk", "rep")),
            P(("blk", "rep"), None, None),
            P(("blk", "rep"), None),
            P(("blk", "rep")),
            P(("blk", "rep"), None),
            P(),
            P(),
            P("rep"),
            P("blk"),
        ),
        out_specs=P("rep", "blk"),
        check_vma=False,
    )
```

time: 506 us -> 134 us (0.26)
  waiting for transfers between devices: 274 us -> 0 us
  blocking collectives: 137 us -> 0 us
  Pallas kernels: 0 us -> 128 us
  local copies, waits for them, and re-layouts: 46 us -> 3.99 us
  starting transfers between devices: 25.4 us -> 0 us
  matrix products: 16.4 us -> 0 us
    all_to_all x3 -> x0, waiting for transfers between devices: 274 us -> none  [the longest x1 274 us: shards(): lax.all_to_all(outbox, 'blk', split_axis=0, concat_axis=0, tiled=True)]
    all_gather x1 -> x0, blocking collectives: 137 us -> none  [shards(): all_ids = lax.all_gather(tile_ids, 'rep', axis=0, tiled=True)]
    pallas_call x0 -> x2, Pallas kernels: none -> 128 us  [the longest x1 126 us: ladder(): pl.pallas_call(functools.partial(ladder_kernel, cell, tuple(groups)), out...]
    all_to_all x3 -> x0, starting transfers between devices: 25.4 us -> none  [the longest x1 13.1 us: shards(): lax.all_to_all(outbox, 'blk', split_axis=0, concat_axis=0, tiled=True)]
    all_to_all x3 -> x0, local copies, waits for them, and re-layouts: 19.4 us -> none  [the longest x1 18.1 us: shards(): lax.all_to_all(outbox, 'blk', split_axis=0, concat_axis=0, tiled=True)]
    dot_general x2 -> x0, matrix products: 16.4 us -> none  [the longest x1 10.1 us: shards(): jnp.einsum('slk,rk->slr', panel_live, amp_live, preferred_element_type=jn...]
    scatter x2 -> x0, local copies, waits for them, and re-layouts: 15.8 us -> none  [the longest x1 14.9 us: shards(): outbox = jnp.zeros((blk_count * capacity, tile_width, row_count), jnp.bfl...]
    broadcast_in_dim x1 -> x0, local copies, waits for them, and re-layouts: 6.04 us -> none  [shards(): jnp.zeros((blk_count * capacity, tile_width, row_count), jnp.bfloat16)]
  transfers between devices with their start and end apart: 3 -> 0, of which waited for: 1 -> 0; matrix products, arithmetic and copies ran while one was open for 4% -> 0% of each run, Pallas kernels for 0% -> 0%
where the time goes in v2:
time: 134 us; the launch traced here: 133 us
  Pallas kernels  128 us (96%)
  local copies, waits for them, and re-layouts  3.99 us (3%)
    pallas_call x1, Pallas kernels, ladder(): pl.pallas_call(functools.partial(ladder_kernel, cell, tuple(groups)), out...  126 us
    unnamed x14, local copies, waits for them, and re-layouts  2.8 us

profile of v2, /device:TPU:1, one launch (start us, length us, event | category | flops | bytes accessed | tf_op | source)
XLA Modules:
  0.0 133.3 jit_solution(10165224338555617812)
XLA Ops:
  0.0 0.0 copy-start.1
  0.0 0.0 copy-start.2
  0.0 0.0 copy-start.3
  0.0 0.0 copy-start.4
  0.0 0.0 copy-start.5
  0.0 0.0 copy-start
  0.0 1.4 %copy.10.owner_ref = s32[43,1]{1,0:T(8,128)} copy(s32[43,1]{0,1:T(1,128)} %param.13) | data formatting | bytes 344 | tf_op args[2]
  1.4 1.4 %copy.11.mask_ref = s32[43,4]{1,0:T(8,128)} copy(s32[43,4]{0,1:T(4,128)} %param.15) | data formatting | bytes 1376 | tf_op args[4]
  2.8 126.4 %shard_map.91 = (f32[3,2,16,16,128]{4,3,2,1,0:T(8,128)S(1)}, f32[8,128]{1,0:T(8,128)}) custom-call(s32[43,1]{1,0:T(8,128)} %copy.10.owner_ref, s32[43]{0:T(128)} %target_ref.1, s32[43,4]{1,0:T(8,128)} %copy.11.mask_ref, s32[1024]{0:T(1024)} %sizes_ref.3, s32[1024]{0:T(1024)} %irreps_ref.1, bf16[256,768]{1,0:T(8,128)(2,1)} %amp_ref.1, ...), custom_call_target="tpu_custom_call" | custom-call | tf_op jit(solution)/shard_map/pallas_call | solution.py:315
  129.3 1.2 slice.3
  131.1 0.0 copy-done.1
  131.1 0.0 copy-done.2
  131.1 0.0 copy-done.3
  131.1 0.0 copy-done.4
  131.1 0.0 copy-done.5
  131.1 0.0 copy-done
  131.2 0.2 conditional.1
  131.4 1.9 %shard_map.92 = bf16[64,3072]{1,0:T(8,128)(2,1)} custom-call(s32[1024]{0:T(1024)S(1)} %copy-done.1, f32[1536,128]{1,0:T(8,128)S(1)} %bitcast.4, f32[1,64]{1,0:T(1,128)} %bitcast.6, f32[1,3072]{1,0:T(1,128)} %bitcast.5), custom_call_target="tpu_custom_call" | custom-call | tf_op jit(solution)/shard_map/pallas_call | solution.py:390
Async XLA Ops:
  0.0 131.1 %copy-start.1 = (s32[1024]{0:T(1024)S(1)}, s32[1024]{0:T(1024)}, u32[]{:S(2)}) copy-start(s32[1024]{0:T(1024)} %sizes_ref.3) | copy-start | bytes 12292
  0.0 131.1 %copy-start.2 = (s32[1024]{0:T(1024)S(1)}, s32[1024]{0:T(1024)}, u32[]{:S(2)}) copy-start(s32[1024]{0:T(1024)} %irreps_ref.1) | copy-start | bytes 12292
  0.0 131.1 %copy-start.3 = (s32[43,4]{0,1:T(4,128)S(1)}, s32[43,4]{0,1:T(4,128)}, u32[]{:S(2)}) copy-start(s32[43,4]{0,1:T(4,128)} %param.15) | copy-start | bytes 2068
  0.0 131.1 %copy-start.4 = (s32[43]{0:T(128)S(1)}, s32[43]{0:T(128)}, u32[]{:S(2)}) copy-start(s32[43]{0:T(128)} %target_ref.1) | copy-start | bytes 520
  0.0 131.1 %copy-start.5 = (s32[43,1]{0,1:T(1,128)S(1)}, s32[43,1]{0,1:T(1,128)}, u32[]{:S(2)}) copy-start(s32[43,1]{0,1:T(1,128)} %param.13) | copy-start | bytes 520
  0.0 131.1 %copy-start = (bf16[256,768]{1,0:T(8,128)(2,1)S(1)}, bf16[256,768]{1,0:T(8,128)(2,1)}, u32[]{:S(2)}) copy-start(bf16[256,768]{1,0:T(8,128)(2,1)} %amp_ref.1) | copy-start | bytes 1179652

commit v3 on v2

--- a/solution.py
+++ b/solution.py
@@ -18,6 +18,13 @@
 OWNED = 16
 SPOTS = NZ * NC * OWNED
 ZT = NC * OWNED
+HALF = R // 2
+PLAN = [
+    ("x", 0), ("y", 1), ("z", 0, 1), ("x", 1), ("z", 0, 2), ("z", 1, 1), ("z", 0, 3), ("z", 1, 2), ("x", 2),
+    ("z", 0, 4), ("z", 1, 3), ("y", 2), ("z", 2, 1), ("x", 3), ("z", 1, 4), ("z", 2, 2), ("z", 3, 1), ("z", 2, 3),
+    ("z", 3, 2), ("x", 4), ("z", 2, 4), ("z", 3, 3), ("z", 4, 1), ("z", 4, 2), ("z", 3, 4), ("z", 4, 3), ("x", 5),
+    ("z", 5, 1), ("z", 4, 4), ("z", 5, 2), ("z", 5, 3), ("z", 5, 4),
+]
 COLUMN = [(dy, dc) for dy in range(NY) for dc in range(NC) if (dy, dc) != (0, 0)]
 
 
@@ -77,11 +84,11 @@
     sources = [irreps_ref[dev * tiles + j] for j in range(tiles)]
 
     def target_of(s):
-        return owner_ref[s, 0] * OWNED + target_ref[s]
+        return owner_ref[s] * OWNED + target_ref[s]
 
     def live_of(s):
         kind = irreps_ref[target_of(s)]
-        return [jnp.where(kind == sources[j], mask_ref[s, j], 0) for j in range(tiles)]
+        return [jnp.where(kind == sources[j], mask_ref[j, s], 0) for j in range(tiles)]
 
     seg_lane = lax.broadcasted_iota(jnp.int32, (8, KPAD), 1)
 
@@ -90,7 +97,6 @@
         value = jnp.where(live[0] + live[1] + live[2] + live[3] > 0, target_of(s) + 1, 0)
         return jnp.where(seg_lane == me * SEG + s, value, row)
 
-    enc[...] = lax.fori_loop(0, slots, encode, jnp.zeros((8, KPAD), jnp.int32))
     lane = lax.broadcasted_iota(jnp.int32, (1, kdim), 1)
 
     def by_tile(vals):
@@ -101,9 +107,6 @@
 
     ends = by_tile([sizes_ref[dev * tiles + j] + j * width for j in range(tiles)])
     amp_v[...] = amp_ref[...] * (lane < ends).astype(jnp.bfloat16)
-    pl.semaphore_wait(barrier, len(peers))
-    icp = start([remote(enc, got.at[me], is_.at[i], ir.at[i], p) for i, (b, p) in enumerate(col)])
-    got[me] = enc[...]
 
     def one(s, carry):
         mask = by_tile(live_of(s)).astype(jnp.bfloat16)
@@ -129,7 +132,13 @@
     for g, (lo, n) in enumerate(groups):
         reads[g].wait()
         lax.fori_loop(lo, lo + n, one, 0)
+        if g == 0:
+            pl.semaphore_wait(barrier, len(peers))
         ycp[0] += y_start(0, g)
+        if g == 1:
+            enc[...] = lax.fori_loop(0, slots, encode, jnp.zeros((8, KPAD), jnp.int32))
+            icp = start([remote(enc, got.at[me], is_.at[i], ir.at[i], p) for i, (b, p) in enumerate(col)])
+            got[me] = enc[...]
     ycp[1] = y_start(1, None)
     own = start([pltpu.make_async_copy(part.at[q, me], yr.at[q, me], own_sem.at[q]) for q in range(CHUNKS)])
 
@@ -172,6 +181,7 @@
 
         lax.fori_loop(0, 8, widen, 0)
 
+    def x_start(q, h):
         def rows(i, carry):
             r = 2 * i
             a = pf[pl.ds(r, KPAD, stride=R), :].astype(jnp.bfloat16)
@@ -183,13 +193,11 @@
             xsend[q, r + 1] = m[:, LANES:]
             return carry
 
-        lax.fori_loop(0, R // 2, rows, 0)
-
-    def x_start(q):
+        lax.fori_loop(h * HALF // 2, (h + 1) * HALF // 2, rows, 0)
         out = []
         for i, p in enumerate(xpeers):
-            cols = pl.ds(i * cell, cell)
-            out.append(remote(xsend.at[q, :, cols], xrecv.at[q, :, cols], xs.at[q, i], xr_sem.at[q, i], p))
+            at = (q, pl.ds(h * HALF, HALF), pl.ds(i * cell, cell))
+            out.append(remote(xsend.at[at], xrecv.at[at], xs.at[q, h, i], xr_sem.at[q, h, i], p))
         return start(out)
 
     def own_part(q):
@@ -202,7 +210,7 @@
 
         lax.fori_loop(0, R // 2, rows, 0)
 
-    def gather(q):
+    def gather(q, h):
         def rows(i, carry):
             r = 2 * i
             p = jnp.concatenate([xrecv[q, r], xrecv[q, r + 1]], axis=1)
@@ -214,87 +222,90 @@
             dense[q, :, r + 1] += d[:, :, LANES:]
             return carry
 
-        lax.fori_loop(0, R // 2, rows, 0)
-
-    half = R // 2
-
-    def z_first(q):
-        far = (z + 4) % NZ
-        zsp[q, 0, :half] = dense[q, far, :half].astype(jnp.bfloat16)
-        zsm[q, 0, half:] = dense[q, far, half:].astype(jnp.bfloat16)
-        lo, hi = pl.ds(0, half), pl.ds(half, half)
-        a = remote(zsp.at[q, 0, lo], zrp.at[q, 0, lo], zps.at[q, 0], zpr.at[q, 0], up)
-        b = remote(zsm.at[q, 0, hi], zrm.at[q, 0, hi], zms.at[q, 0], zmr.at[q, 0], down)
-        start([a, b])
-        return a, b
-
-    def z_step(q, t, before):
-        a, b = before
-        dp, dm = (z + 4 - t) % NZ, (z + 4 + t) % NZ
-        a.wait()
-        if t == 1:
-            zsp[q, t, :half] = (dense[q, dp, :half] + zrp[q, 0, :half].astype(jnp.float32)).astype(jnp.bfloat16)
-            zsp[q, t, half:] = dense[q, dp, half:].astype(jnp.bfloat16)
-        else:
-            zsp[q, t] = (dense[q, dp] + zrp[q, t - 1].astype(jnp.float32)).astype(jnp.bfloat16)
-        a = remote(zsp.at[q, t], zrp.at[q, t], zps.at[q, t], zpr.at[q, t], up)
-        a.start()
-        b.wait()
-        if t == 1:
-            zsm[q, t, half:] = (dense[q, dm, half:] + zrm[q, 0, half:].astype(jnp.float32)).astype(jnp.bfloat16)
-            zsm[q, t, :half] = dense[q, dm, :half].astype(jnp.bfloat16)
-        else:
-            zsm[q, t] = (dense[q, dm] + zrm[q, t - 1].astype(jnp.float32)).astype(jnp.bfloat16)
-        b = remote(zsm.at[q, t], zrm.at[q, t], zms.at[q, t], zmr.at[q, t], down)
-        b.start()
-        return a, b
-
-    def z_last(q, before):
-        wait(before)
-        f = dense[q, z] + zrp[q, 3].astype(jnp.float32) + zrm[q, 3].astype(jnp.float32)
-        fx[q, 0] = f[:, :OWNED]
-        fx[q, 1] = f[:, OWNED:]
-        cp = remote(fx.at[q, 1 - c], fr.at[q], cs.at[q], cr.at[q], partner)
-        cp.start()
-        return cp
-
-    def z_all(q):
-        st = z_first(q)
-        for t in range(1, 4):
-            st = z_step(q, t, st)
-        return z_last(q, st)
-
-    xcp, last = {}, {}
-    for q in range(CHUNKS):
+        lax.fori_loop(h * HALF // 2, (h + 1) * HALF // 2, rows, 0)
+
+    def z_step(q, h, t):
+        lo, mid, hi = h * HALF, h * HALF + HALF // 2, (h + 1) * HALF
+        all_rows, first, second = slice(lo, hi), slice(lo, mid), slice(mid, hi)
+        ways = (
+            (zsp, zrp, zps, zpr, up, (z + 4 - t) % NZ, first, second),
+            (zsm, zrm, zms, zmr, down, (z + 4 + t) % NZ, second, first),
+        )
+        out = []
+        for w, (zs, zr, ss, rs, peer, d, near, rest) in enumerate(ways):
+            if t > 0:
+                zcp[q, h][w].wait()
+            if t == 0:
+                zs[q, 0, near] = dense[q, d, near].astype(jnp.bfloat16)
+                at = (q, 0, pl.ds(near.start, HALF // 2))
+            else:
+                at = (q, t, pl.ds(lo, HALF))
+                if t == 1:
+                    zs[q, 1, near] = (dense[q, d, near] + zr[q, 0, near].astype(jnp.float32)).astype(jnp.bfloat16)
+                    zs[q, 1, rest] = dense[q, d, rest].astype(jnp.bfloat16)
+                else:
+                    both = dense[q, d, all_rows] + zr[q, t - 1, all_rows].astype(jnp.float32)
+                    zs[q, t, all_rows] = both.astype(jnp.bfloat16)
+            out.append(remote(zs.at[at], zr.at[at], ss.at[q, h, t], rs.at[q, h, t], peer))
+            out[-1].start()
+        zcp[q, h] = out
+
+    def z_last(q, h):
+        wait(zcp[q, h])
+        at = slice(h * HALF, (h + 1) * HALF)
+        f = dense[q, z, at] + zrp[q, 3, at].astype(jnp.float32) + zrm[q, 3, at].astype(jnp.float32)
+        fx[q, 0, at] = f[:, :OWNED]
+        fx[q, 1, at] = f[:, OWNED:]
+        span = pl.ds(h * HALF, HALF)
+        last[q, h] = remote(fx.at[q, 1 - c, span], fr.at[q, span], cs.at[q, h], cr.at[q, h], partner)
+        last[q, h].start()
+
+    xcp, zcp, last = {}, {}, {}
+
+    def take_y(q):
         wait(ycp[q])
         own[q].wait()
         if q + 2 < CHUNKS:
             ycp[q + 2] = y_start(q + 2, None)
         merge(q)
-        xcp[q] = x_start(q)
+        for h in range(2):
+            xcp[q, h] = x_start(q, h)
         own_part(q)
-        if q == 0:
-            wait(jcp)
-            nth = (lax.broadcasted_iota(jnp.int32, (SPOTS, cell), 1) + 1).astype(jnp.float32)
-            for i in range(NX - 1):
-                _, rank = ranks(xids[i, 0:1, :], x)
-                tmat[i] = (rank[:, 0:1] == nth).astype(jnp.bfloat16)
-            wait(kcp)
-            cnt[...] = jnp.max(zcnt[...], axis=0)
-            lcp = start([remote(cnt, xcnt.at[x], ls.at[i], lr.at[i], p) for i, p in enumerate(xpeers)])
-            xcnt[x] = cnt[...]
-        if q >= 1:
-            wait(xcp[q - 1])
-            gather(q - 1)
-            last[q - 1] = z_all(q - 1)
-    q = CHUNKS - 1
+
+    def take_x(q, h):
+        wait(xcp[q, h])
+        gather(q, h)
+        z_step(q, h, 0)
+
+    def zstep(u, t):
+        q, h = u // 2, u % 2
+        if t < 4:
+            z_step(q, h, t)
+        else:
+            z_last(q, h)
+
+    take_y(0)
+    wait(jcp)
+    nth = (lax.broadcasted_iota(jnp.int32, (SPOTS, cell), 1) + 1).astype(jnp.float32)
+    for i in range(NX - 1):
+        _, rank = ranks(xids[i, 0:1, :], x)
+        tmat[i] = (rank[:, 0:1] == nth).astype(jnp.bfloat16)
+    wait(kcp)
+    cnt[...] = jnp.max(zcnt[...], axis=0)
+    lcp = start([remote(cnt, xcnt.at[x], ls.at[i], lr.at[i], p) for i, p in enumerate(xpeers)])
+    xcnt[x] = cnt[...]
+    for step in PLAN:
+        if step[0] == "y":
+            take_y(step[1])
+        elif step[0] == "x":
+            take_x(step[1] // 2, step[1] % 2)
+        else:
+            zstep(step[1], step[2])
     wait(lcp)
     most_ref[...] = jnp.max(xcnt[...], axis=0)
-    wait(xcp[q])
-    gather(q)
-    last[q] = z_all(q)
     for q in range(CHUNKS):
-        last[q].wait()
+        for h in range(2):
+            last[q, h].wait()
         out_ref[q, c] = fx[q, c]
         out_ref[q, 1 - c] = fr[q]
 
@@ -303,7 +314,7 @@
     slots = panels.shape[0]
     groups, lo = [], 0
     while lo < slots:
-        n = min(11, slots - lo)
+        n = min(13 if groups else 5, slots - lo)
         groups.append((lo, n))
         lo += n
     ng = len(groups)
@@ -345,10 +356,10 @@
             pltpu.VMEM((NX, 8, LANES), f32),
             dma((ng,)), dma((CHUNKS,)),
             dma((CHUNKS, ng, 7)), dma((CHUNKS, ng, 7)),
-            dma((CHUNKS, 3)), dma((CHUNKS, 3)),
-            dma((CHUNKS, 4)), dma((CHUNKS, 4)),
-            dma((CHUNKS, 4)), dma((CHUNKS, 4)),
-            dma((CHUNKS,)), dma((CHUNKS,)),
+            dma((CHUNKS, 2, 3)), dma((CHUNKS, 2, 3)),
+            dma((CHUNKS, 2, 4)), dma((CHUNKS, 2, 4)),
+            dma((CHUNKS, 2, 4)), dma((CHUNKS, 2, 4)),
+            dma((CHUNKS, 2)), dma((CHUNKS, 2)),
             dma((7,)), dma((7,)),
             dma((3,)), dma((3,)),
             dma((7,)), dma((7,)),
@@ -406,7 +417,7 @@
     occ_energy,
     vir_energy,
 ):
-    args = (panel_owner_index, panel_target_tile, panel_tile_mask, tile_sizes, tile_irreps, amplitudes, panels)
+    args = (panel_owner_index[:, 0], panel_target_tile, panel_tile_mask.T, tile_sizes, tile_irreps, amplitudes, panels)
     summed, most = ladder(CELL, 0, *args)
     summed = lax.cond(
         most[0, 0] <= CELL,

time: 134 us -> 119 us (0.89)
  Pallas kernels: 128 us -> 117 us
  local copies, waits for them, and re-layouts: 3.99 us -> 1.21 us
    pallas_call x1, Pallas kernels: 126 us -> 115 us  [ladder(): pl.pallas_call(functools.partial(ladder_kernel, cell, tuple(groups)), out...]
    unnamed x14 -> x12, local copies, waits for them, and re-layouts: 2.8 us -> 0.02 us
where the time goes in v3:
time: 119 us
  Pallas kernels  117 us (98%)
  local copies, waits for them, and re-layouts  1.21 us (1%)
    pallas_call x1, Pallas kernels, ladder(): pl.pallas_call(functools.partial(ladder_kernel, cell, tuple(groups)), out...  115 us

profile of v3, /device:TPU:1, one launch (start us, length us, event | category | flops | bytes accessed | tf_op | source)
XLA Modules:
  0.0 119.3 jit_solution(11978865523241428722)
XLA Ops:
  0.0 0.0 copy-start.1
  0.0 0.0 copy-start.2
  0.0 0.0 copy-start.5
  0.0 0.0 copy-start
  0.0 0.0 copy-start.3
  0.0 0.0 copy-start.4
  0.0 115.2 %shard_map.91 = (f32[3,2,16,16,128]{4,3,2,1,0:T(8,128)S(1)}, f32[8,128]{1,0:T(8,128)}) custom-call(s32[43]{0:T(128)} %bitcast.10, s32[43]{0:T(128)} %target_ref.1, s32[4,43]{1,0:T(4,128)} %bitcast.8, s32[1024]{0:T(1024)} %sizes_ref.3, s32[1024]{0:T(1024)} %irreps_ref.1, bf16[256,768]{1,0:T(8,128)(2,1)} %amp_ref.1, bf16[43,192,768]{2,1,0:T(8,128)(2,1)} %panels_hbm.1), custom_call_target="tpu_custom_call" | custom-call | tf_op jit(solution)/shard_map/pallas_call | solution.py:326
  115.3 1.2 slice.3
  117.1 0.0 copy-done.1
  117.1 0.0 copy-done.2
  117.1 0.0 copy-done.5
  117.1 0.0 copy-done
  117.2 0.0 copy-done.3
  117.2 0.0 copy-done.4
  117.2 0.2 conditional.1
  117.4 1.9 %shard_map.92 = bf16[64,3072]{1,0:T(8,128)(2,1)} custom-call(s32[1024]{0:T(1024)S(1)} %copy-done.1, f32[1536,128]{1,0:T(8,128)S(1)} %bitcast.6, f32[1,64]{1,0:T(1,128)} %bitcast.12, f32[1,3072]{1,0:T(1,128)} %bitcast.7), custom_call_target="tpu_custom_call" | custom-call | tf_op jit(solution)/shard_map/pallas_call | solution.py:401
Async XLA Ops:
  0.0 117.1 %copy-start.1 = (s32[1024]{0:T(1024)S(1)}, s32[1024]{0:T(1024)}, u32[]{:S(2)}) copy-start(s32[1024]{0:T(1024)} %sizes_ref.3) | copy-start | bytes 12292
  0.0 117.1 %copy-start.2 = (s32[1024]{0:T(1024)S(1)}, s32[1024]{0:T(1024)}, u32[]{:S(2)}) copy-start(s32[1024]{0:T(1024)} %irreps_ref.1) | copy-start | bytes 12292
  0.0 117.1 %copy-start.5 = (s32[43]{0:T(128)S(1)}, s32[43]{0:T(128)}, u32[]{:S(2)}) copy-start(s32[43]{0:T(128)} %target_ref.1) | copy-start | bytes 520
  0.0 117.1 %copy-start = (bf16[256,768]{1,0:T(8,128)(2,1)S(1)}, bf16[256,768]{1,0:T(8,128)(2,1)}, u32[]{:S(2)}) copy-start(bf16[256,768]{1,0:T(8,128)(2,1)} %amp_ref.1) | copy-start | bytes 1179652
  0.0 117.1 %copy-start.3 = (s32[43,4]{0,1:T(4,128)S(1)}, s32[43,4]{0,1:T(4,128)}, u32[]{:S(2)}) copy-start(s32[43,4]{0,1:T(4,128)} %param.15) | copy-start | bytes 2068
  0.0 117.1 %copy-start.4 = (s32[43,1]{0,1:T(1,128)S(1)}, s32[43,1]{0,1:T(1,128)}, u32[]{:S(2)}) copy-start(s32[43,1]{0,1:T(1,128)} %param.13) | copy-start | bytes 520

commit v4 on v3

--- a/solution.py
+++ b/solution.py
@@ -18,13 +18,12 @@
 OWNED = 16
 SPOTS = NZ * NC * OWNED
 ZT = NC * OWNED
-HALF = R // 2
-PLAN = [
-    ("x", 0), ("y", 1), ("z", 0, 1), ("x", 1), ("z", 0, 2), ("z", 1, 1), ("z", 0, 3), ("z", 1, 2), ("x", 2),
-    ("z", 0, 4), ("z", 1, 3), ("y", 2), ("z", 2, 1), ("x", 3), ("z", 1, 4), ("z", 2, 2), ("z", 3, 1), ("z", 2, 3),
-    ("z", 3, 2), ("x", 4), ("z", 2, 4), ("z", 3, 3), ("z", 4, 1), ("z", 4, 2), ("z", 3, 4), ("z", 4, 3), ("x", 5),
-    ("z", 5, 1), ("z", 4, 4), ("z", 5, 2), ("z", 5, 3), ("z", 5, 4),
-]
+UNITS = ((0, 0, 16), (1, 0, 16), (2, 0, 8), (2, 8, 8))
+NU = len(UNITS)
+PLAN = (
+    ['s', 'y1', 'm1', 'x0', 'z01', 'z02', 'y2', 'm2', 'm3', 'z03', 'z04', 'x1', 'z11', 'z12', 'z13']
+    + ['x2', 'x3', 'z14', 'z21', 'z31', 'z22', 'z32', 'z23', 'z33', 'z24', 'z34']
+)
 COLUMN = [(dy, dc) for dy in range(NY) for dc in range(NC) if (dy, dc) != (0, 0)]
 
 
@@ -56,7 +55,8 @@
 
 def ladder_kernel(
     cell, groups,
-    owner_ref, target_ref, mask_ref, sizes_ref, irreps_ref, amp_ref, panels_hbm, out_ref, most_ref,
+    owner_in, target_in, mask_in, sizes_in, irreps_in, amp_in, panels_hbm, out_ref, most_ref,
+    owner_ref, target_ref, mask_ref, sizes_ref, irreps_ref, amp_ref, first_sem,
     panels_v, amp_v, part, yr, pf, pb, smat, sown, tmat, xsend, xrecv, dense,
     zsp, zrp, zsm, zrm, fx, fr, enc, got, mine, xids, cnt, zcnt, xcnt,
     in_sem, own_sem, ys, yr_sem, xs, xr_sem, zps, zpr, zms, zmr, cs, cr,
@@ -67,10 +67,6 @@
     dev = lax.axis_index("blk") * NY + y
     slots, width, kdim = panels_v.shape
     tiles = kdim // width
-    reads = start([
-        pltpu.make_async_copy(panels_hbm.at[pl.ds(lo, n)], panels_v.at[pl.ds(lo, n)], in_sem.at[g])
-        for g, (lo, n) in enumerate(groups)
-    ])
     col = [(((y + dy) % NY) * NC + (c + dc) % NC, device(x, z, (c + dc) % NC, (y + dy) % NY)) for dy, dc in COLUMN]
     xpeers = [device((x + d) % NX, z, c, y) for d in range(1, NX)]
     zpeers = [device(x, (z + d) % NZ, c, y) for d in range(1, NZ)]
@@ -80,6 +76,19 @@
     peers = [p for _, p in col] + xpeers + zpeers
     for p in peers:
         pl.semaphore_signal(barrier, inc=1, device_id=p, device_id_type=MESH)
+
+    small = start([
+        pltpu.make_async_copy(a, b, first_sem.at[i])
+        for i, (a, b) in enumerate((
+            (amp_in, amp_ref), (owner_in, owner_ref), (target_in, target_ref),
+            (mask_in, mask_ref), (sizes_in, sizes_ref), (irreps_in, irreps_ref),
+        ))
+    ])
+    reads = start([
+        pltpu.make_async_copy(panels_hbm.at[pl.ds(lo, n)], panels_v.at[pl.ds(lo, n)], in_sem.at[g])
+        for g, (lo, n) in enumerate(groups)
+    ])
+    wait(small)
 
     sources = [irreps_ref[dev * tiles + j] for j in range(tiles)]
 
@@ -120,26 +129,27 @@
         part[2, :, s] = jnp.concatenate([high[:, :R], high[:, R:]], axis=-1).astype(jnp.bfloat16)
         return carry
 
-    def y_start(q, g):
-        lo, n = groups[g] if g is not None else (0, slots)
-        k = g if g is not None else 0
-        return start([
+    halves = ((0, (slots + 1) // 2), ((slots + 1) // 2, slots // 2))
+
+    def y_start(q, k):
+        lo, n = groups[k] if q == 0 else halves[k]
+        ycp[q, k] = start([
             remote(part.at[q, b, pl.ds(lo, n)], yr.at[q, me, pl.ds(lo, n)], ys.at[q, k, i], yr_sem.at[q, k, i], p)
             for i, (b, p) in enumerate(col)
         ])
 
-    ycp = {0: []}
+    ycp = {}
     for g, (lo, n) in enumerate(groups):
         reads[g].wait()
         lax.fori_loop(lo, lo + n, one, 0)
         if g == 0:
             pl.semaphore_wait(barrier, len(peers))
-        ycp[0] += y_start(0, g)
+        y_start(0, g)
         if g == 1:
             enc[...] = lax.fori_loop(0, slots, encode, jnp.zeros((8, KPAD), jnp.int32))
             icp = start([remote(enc, got.at[me], is_.at[i], ir.at[i], p) for i, (b, p) in enumerate(col)])
             got[me] = enc[...]
-    ycp[1] = y_start(1, None)
+    y_start(1, 0)
     own = start([pltpu.make_async_copy(part.at[q, me], yr.at[q, me], own_sem.at[q]) for q in range(CHUNKS)])
 
     wait(icp)
@@ -181,7 +191,9 @@
 
         lax.fori_loop(0, 8, widen, 0)
 
-    def x_start(q, h):
+    def x_start(u):
+        q, lo, n = UNITS[u]
+
         def rows(i, carry):
             r = 2 * i
             a = pf[pl.ds(r, KPAD, stride=R), :].astype(jnp.bfloat16)
@@ -193,24 +205,25 @@
             xsend[q, r + 1] = m[:, LANES:]
             return carry
 
-        lax.fori_loop(h * HALF // 2, (h + 1) * HALF // 2, rows, 0)
+        lax.fori_loop(lo // 2, (lo + n) // 2, rows, 0)
         out = []
         for i, p in enumerate(xpeers):
-            at = (q, pl.ds(h * HALF, HALF), pl.ds(i * cell, cell))
-            out.append(remote(xsend.at[at], xrecv.at[at], xs.at[q, h, i], xr_sem.at[q, h, i], p))
-        return start(out)
-
-    def own_part(q):
-        def rows(i, carry):
+            at = (q, pl.ds(lo, n), pl.ds(i * cell, cell))
+            out.append(remote(xsend.at[at], xrecv.at[at], xs.at[u, i], xr_sem.at[u, i], p))
+        xcp[u] = start(out)
+
+        def own_rows(i, carry):
             r = 2 * i
             d = jnp.dot(sown[...], pb[i], preferred_element_type=jnp.float32).reshape(NZ, ZT, 2 * LANES)
             dense[q, :, r] = d[:, :, :LANES]
             dense[q, :, r + 1] = d[:, :, LANES:]
             return carry
 
-        lax.fori_loop(0, R // 2, rows, 0)
-
-    def gather(q, h):
+        lax.fori_loop(lo // 2, (lo + n) // 2, own_rows, 0)
+
+    def gather(u):
+        q, lo, n = UNITS[u]
+
         def rows(i, carry):
             r = 2 * i
             p = jnp.concatenate([xrecv[q, r], xrecv[q, r + 1]], axis=1)
@@ -222,10 +235,11 @@
             dense[q, :, r + 1] += d[:, :, LANES:]
             return carry
 
-        lax.fori_loop(h * HALF // 2, (h + 1) * HALF // 2, rows, 0)
-
-    def z_step(q, h, t):
-        lo, mid, hi = h * HALF, h * HALF + HALF // 2, (h + 1) * HALF
+        lax.fori_loop(lo // 2, (lo + n) // 2, rows, 0)
+
+    def z_step(u, t):
+        q, lo, n = UNITS[u]
+        mid, hi = lo + n // 2, lo + n
         all_rows, first, second = slice(lo, hi), slice(lo, mid), slice(mid, hi)
         ways = (
             (zsp, zrp, zps, zpr, up, (z + 4 - t) % NZ, first, second),
@@ -234,57 +248,65 @@
         out = []
         for w, (zs, zr, ss, rs, peer, d, near, rest) in enumerate(ways):
             if t > 0:
-                zcp[q, h][w].wait()
+                zcp[u][w].wait()
             if t == 0:
                 zs[q, 0, near] = dense[q, d, near].astype(jnp.bfloat16)
-                at = (q, 0, pl.ds(near.start, HALF // 2))
+                at = (q, 0, pl.ds(near.start, n // 2))
             else:
-                at = (q, t, pl.ds(lo, HALF))
+                at = (q, t, pl.ds(lo, n))
                 if t == 1:
                     zs[q, 1, near] = (dense[q, d, near] + zr[q, 0, near].astype(jnp.float32)).astype(jnp.bfloat16)
                     zs[q, 1, rest] = dense[q, d, rest].astype(jnp.bfloat16)
                 else:
                     both = dense[q, d, all_rows] + zr[q, t - 1, all_rows].astype(jnp.float32)
                     zs[q, t, all_rows] = both.astype(jnp.bfloat16)
-            out.append(remote(zs.at[at], zr.at[at], ss.at[q, h, t], rs.at[q, h, t], peer))
+            out.append(remote(zs.at[at], zr.at[at], ss.at[u, t], rs.at[u, t], peer))
             out[-1].start()
-        zcp[q, h] = out
-
-    def z_last(q, h):
-        wait(zcp[q, h])
-        at = slice(h * HALF, (h + 1) * HALF)
+        zcp[u] = out
+
+    def z_last(u):
+        q, lo, n = UNITS[u]
+        wait(zcp[u])
+        at = slice(lo, lo + n)
         f = dense[q, z, at] + zrp[q, 3, at].astype(jnp.float32) + zrm[q, 3, at].astype(jnp.float32)
         fx[q, 0, at] = f[:, :OWNED]
         fx[q, 1, at] = f[:, OWNED:]
-        span = pl.ds(h * HALF, HALF)
-        last[q, h] = remote(fx.at[q, 1 - c, span], fr.at[q, span], cs.at[q, h], cr.at[q, h], partner)
-        last[q, h].start()
+        span = pl.ds(lo, n)
+        last[u] = remote(fx.at[q, 1 - c, span], fr.at[q, span], cs.at[u], cr.at[u], partner)
+        last[u].start()
 
     xcp, zcp, last = {}, {}, {}
 
     def take_y(q):
-        wait(ycp[q])
+        if q == 0:
+            for g in range(len(groups) - 1):
+                wait(ycp[0, g])
+            y_start(1, 1)
+            wait(ycp[0, len(groups) - 1])
+        else:
+            if q > 1:
+                wait(ycp[q, 0])
+            wait(ycp[q, 1])
+            if q + 1 < CHUNKS:
+                y_start(q + 1, 1)
         own[q].wait()
-        if q + 2 < CHUNKS:
-            ycp[q + 2] = y_start(q + 2, None)
         merge(q)
-        for h in range(2):
-            xcp[q, h] = x_start(q, h)
-        own_part(q)
-
-    def take_x(q, h):
-        wait(xcp[q, h])
-        gather(q, h)
-        z_step(q, h, 0)
+
+    def take_x(u):
+        wait(xcp[u])
+        gather(u)
+        z_step(u, 0)
 
     def zstep(u, t):
-        q, h = u // 2, u % 2
         if t < 4:
-            z_step(q, h, t)
+            z_step(u, t)
         else:
-            z_last(q, h)
+            z_last(u)
 
     take_y(0)
+    for u in range(NU):
+        if UNITS[u][0] == 0:
+            x_start(u)
     wait(jcp)
     nth = (lax.broadcasted_iota(jnp.int32, (SPOTS, cell), 1) + 1).astype(jnp.float32)
     for i in range(NX - 1):
@@ -295,17 +317,22 @@
     lcp = start([remote(cnt, xcnt.at[x], ls.at[i], lr.at[i], p) for i, p in enumerate(xpeers)])
     xcnt[x] = cnt[...]
     for step in PLAN:
-        if step[0] == "y":
-            take_y(step[1])
-        elif step[0] == "x":
-            take_x(step[1] // 2, step[1] % 2)
+        kind, at = step[0], [int(v) for v in step[1:]]
+        if kind == "s":
+            wait(ycp[1, 0])
+            y_start(2, 0)
+        elif kind == "y":
+            take_y(at[0])
+        elif kind == "m":
+            x_start(at[0])
+        elif kind == "x":
+            take_x(at[0])
         else:
-            zstep(step[1], step[2])
+            zstep(*at)
     wait(lcp)
     most_ref[...] = jnp.max(xcnt[...], axis=0)
+    wait([last[u] for u in range(NU)])
     for q in range(CHUNKS):
-        for h in range(2):
-            last[q, h].wait()
         out_ref[q, c] = fx[q, c]
         out_ref[q, 1 - c] = fr[q]
 
@@ -319,7 +346,6 @@
         lo += n
     ng = len(groups)
     vmem = pl.BlockSpec(memory_space=pltpu.VMEM)
-    smem = pl.BlockSpec(memory_space=pltpu.SMEM)
     dma = pltpu.SemaphoreType.DMA
     bf, f32, i32 = jnp.bfloat16, jnp.float32, jnp.int32
     zbuf = pltpu.VMEM((CHUNKS, 4, R, ZT, LANES), bf)
@@ -329,9 +355,16 @@
             jax.ShapeDtypeStruct((CHUNKS, NC, R, OWNED, LANES), f32),
             jax.ShapeDtypeStruct((8, LANES), f32),
         ),
-        in_specs=[smem] * 5 + [vmem, pl.BlockSpec(memory_space=pl.ANY)],
+        in_specs=[pl.BlockSpec(memory_space=pl.ANY)] * 7,
         out_specs=(vmem, vmem),
         scratch_shapes=[
+            pltpu.SMEM(owner.shape, i32),
+            pltpu.SMEM(target.shape, i32),
+            pltpu.SMEM(mask.shape, i32),
+            pltpu.SMEM(sizes.shape, i32),
+            pltpu.SMEM(irreps.shape, i32),
+            pltpu.VMEM(amplitudes.shape, bf),
+            dma((6,)),
             pltpu.VMEM(panels.shape, bf),
             pltpu.VMEM(amplitudes.shape, bf),
             pltpu.VMEM((CHUNKS, 8, slots, R, LANES), bf),
@@ -356,10 +389,10 @@
             pltpu.VMEM((NX, 8, LANES), f32),
             dma((ng,)), dma((CHUNKS,)),
             dma((CHUNKS, ng, 7)), dma((CHUNKS, ng, 7)),
-            dma((CHUNKS, 2, 3)), dma((CHUNKS, 2, 3)),
-            dma((CHUNKS, 2, 4)), dma((CHUNKS, 2, 4)),
-            dma((CHUNKS, 2, 4)), dma((CHUNKS, 2, 4)),
-            dma((CHUNKS, 2)), dma((CHUNKS, 2)),
+            dma((NU, 3)), dma((NU, 3)),
+            dma((NU, 4)), dma((NU, 4)),
+            dma((NU, 4)), dma((NU, 4)),
+            dma((NU,)), dma((NU,)),
             dma((7,)), dma((7,)),
             dma((3,)), dma((3,)),
             dma((7,)), dma((7,)),

time: 119 us -> 118 us (level)
    pallas_call x1, Pallas kernels: 115 us -> 114 us  [ladder(): pl.pallas_call(functools.partial(ladder_kernel, cell, tuple(groups)), out...]
where the time goes in v4:
time: 118 us
  Pallas kernels  116 us (98%)
  local copies, waits for them, and re-layouts  1.21 us (1%)
    pallas_call x1, Pallas kernels, ladder(): pl.pallas_call(functools.partial(ladder_kernel, cell, tuple(groups)), out...  114 us

profile of v4, /device:TPU:1, one launch (start us, length us, event | category | flops | bytes accessed | tf_op | source)
XLA Modules:
  0.0 117.9 jit_solution(4757188868252298043)
XLA Ops:
  0.0 0.0 copy-start.1
  0.0 0.0 copy-start.2
  0.0 0.0 copy-start.5
  0.0 0.0 copy-start
  0.0 0.0 copy-start.3
  0.0 0.0 copy-start.4
  0.0 113.8 %shard_map.91 = (f32[3,2,16,16,128]{4,3,2,1,0:T(8,128)S(1)}, f32[8,128]{1,0:T(8,128)}) custom-call(s32[43]{0:T(128)} %bitcast.10, s32[43]{0:T(128)} %target_in.1, s32[4,43]{1,0:T(4,128)} %bitcast.8, s32[1024]{0:T(1024)} %sizes_ref.1, s32[1024]{0:T(1024)} %irreps_in.1, bf16[256,768]{1,0:T(8,128)(2,1)} %amp_in.1, bf16[43,192,768]{2,1,0:T(8,128)(2,1)} %panels_hbm.1), custom_call_target="tpu_custom_call" | custom-call | tf_op jit(solution)/shard_map/pallas_call | solution.py:352
  113.9 1.2 %slice.3 = f32[1,1]{1,0:T(1,128)} slice(f32[8,128]{1,0:T(8,128)} %get-tuple-element.33), slice={[0:1], [0:1]} | slice | bytes 8 | tf_op jit(solution)/shard_map/slice | solution.py:456
  115.7 0.0 copy-done.1
  115.7 0.0 copy-done.2
  115.7 0.0 copy-done.5
  115.7 0.0 copy-done
  115.7 0.0 copy-done.3
  115.8 0.0 copy-done.4
  115.8 0.2 conditional.1
  116.0 1.9 %shard_map.92 = bf16[64,3072]{1,0:T(8,128)(2,1)} custom-call(s32[1024]{0:T(1024)S(1)} %copy-done.1, f32[1536,128]{1,0:T(8,128)S(1)} %bitcast.6, f32[1,64]{1,0:T(1,128)} %bitcast.12, f32[1,3072]{1,0:T(1,128)} %bitcast.7), custom_call_target="tpu_custom_call" | custom-call | tf_op jit(solution)/shard_map/pallas_call | solution.py:434
Async XLA Ops:
  0.0 115.7 %copy-start.1 = (s32[1024]{0:T(1024)S(1)}, s32[1024]{0:T(1024)}, u32[]{:S(2)}) copy-start(s32[1024]{0:T(1024)} %sizes_ref.1) | copy-start | bytes 12292
  0.0 115.7 %copy-start.2 = (s32[1024]{0:T(1024)S(1)}, s32[1024]{0:T(1024)}, u32[]{:S(2)}) copy-start(s32[1024]{0:T(1024)} %irreps_in.1) | copy-start | bytes 12292
  0.0 115.7 %copy-start.5 = (s32[43]{0:T(128)S(1)}, s32[43]{0:T(128)}, u32[]{:S(2)}) copy-start(s32[43]{0:T(128)} %target_in.1) | copy-start | bytes 520
  0.0 115.7 %copy-start = (bf16[256,768]{1,0:T(8,128)(2,1)S(1)}, bf16[256,768]{1,0:T(8,128)(2,1)}, u32[]{:S(2)}) copy-start(bf16[256,768]{1,0:T(8,128)(2,1)} %amp_in.1) | copy-start | bytes 1179652
  0.0 115.7 %copy-start.3 = (s32[43,4]{0,1:T(4,128)S(1)}, s32[43,4]{0,1:T(4,128)}, u32[]{:S(2)}) copy-start(s32[43,4]{0,1:T(4,128)} %param.15) | copy-start | bytes 2068
  0.0 115.7 %copy-start.4 = (s32[43,1]{0,1:T(1,128)S(1)}, s32[43,1]{0,1:T(1,128)}, u32[]{:S(2)}) copy-start(s32[43,1]{0,1:T(1,128)} %param.13) | copy-start | bytes 520
